TPU v7x, 32 devices: a whole 2x2x4 slice. The times are simulated.
32 devices in a mesh: ctx: 8 (over z, y), head: 4 (over x, core).
Axes of the slice: x: 2, y: 2, z: 4, core: 2. Of those that a mesh axis runs over, the one named last changes fastest.
Arguments:
- queries: bfloat16 [1280, 8192], P('ctx', 'head'), may hold values from -6 to 6
- keys: bfloat16 [1280, 2048], P('ctx', 'head'), may hold values from -6 to 6
- values: bfloat16 [1280, 2048], P('ctx', 'head'), may hold values from -6 to 6
- out_grad: bfloat16 [1280, 8192], P('ctx', 'head'), may hold values from -6 to 6
- order: int32 [16], replicated, may hold values from 0 to 15, as said below
Outputs:
- attention: bfloat16 [1280, 8192], P('ctx', 'head')
- grad_queries: bfloat16 [1280, 8192], P('ctx', 'head')
- grad_keys: bfloat16 [1280, 2048], P('ctx', 'head')
- grad_values: bfloat16 [1280, 2048], P('ctx', 'head')
Inputs may be any that keep to these rules, and one draw needn't show every extreme that they name: order is a permutation of the 16 spans; row blocks 2i and 2i + 1 (the rows of index i of ctx) hold spans c and 15 - c for some c, in either order.
All inputs are finite; a program needn't handle non-finite values.
Results may differ from a plain program's by a relative error of at most 0.03.
Values may be sent and summed in bfloat16 or wider, within the bound.
A program may use at most 64 MiB of HBM per device.

v0:
```python
import math

import jax
import jax.numpy as jnp
from jax import lax
from jax.sharding import PartitionSpec as P

HEADS = 32
KV_HEADS = 8
HEAD_DIM = 128


NEG = -1e30


def shifted(array, axis, by):
    length = lax.axis_size(axis)
    return lax.ppermute(array, axis, [(i, (i + by) % length) for i in range(length)])


def attend(carry_state, q_part, q_pos, k_part, v_part, k_pos, score_scale):
    row_top, row_total, weighted = carry_state
    scores = (
        jnp.einsum("acxgd,bsxd->axgcbs", q_part, k_part, preferred_element_type=jnp.float32)
        * score_scale
    )
    visible = k_pos[None, None, None, None, :, :] <= q_pos[:, None, None, :, None, None]
    scores = jnp.where(visible, scores, NEG)
    block_top = jnp.max(scores, axis=5)
    block_weights = jnp.where(visible, jnp.exp(scores - block_top[..., None]), 0.0)
    block_total = jnp.sum(block_weights, axis=5)
    block_sums = jnp.einsum(
        "axgcbs,bsxd->axgcbd",
        block_weights.astype(jnp.bfloat16),
        v_part,
        preferred_element_type=jnp.float32,
    )
    new_top = jnp.maximum(row_top, jnp.max(block_top, axis=4))
    rescale = jnp.exp(row_top - new_top)
    block_factor = jnp.exp(block_top - new_top[..., None])
    row_total = row_total * rescale + jnp.sum(block_factor * block_total, axis=4)
    weighted = weighted * rescale[..., None] + jnp.sum(block_factor[..., None] * block_sums, axis=4)
    return (new_top, row_total, weighted)


def attend_back(q_part, g_part, log_total, row_dot, q_pos, k_part, v_part, k_pos, score_scale):
    scores = (
        jnp.einsum("acxgd,bsxd->axgcbs", q_part, k_part, preferred_element_type=jnp.float32)
        * score_scale
    )
    visible = k_pos[None, None, None, None, :, :] <= q_pos[:, None, None, :, None, None]
    probs = jnp.where(
        visible, jnp.exp(jnp.where(visible, scores, NEG) - log_total[..., None, None]), 0.0
    )
    grad_value = jnp.einsum(
        "axgcbs,acxgd->bsxd", probs.astype(jnp.bfloat16), g_part, preferred_element_type=jnp.float32
    )
    grad_probs = jnp.einsum(
        "acxgd,bsxd->axgcbs", g_part, v_part, preferred_element_type=jnp.float32
    )
    grad_scores = (probs * (grad_probs - row_dot[..., None, None])).astype(jnp.bfloat16)
    grad_query = jnp.einsum(
        "axgcbs,bsxd->acxgd", grad_scores, k_part, preferred_element_type=jnp.float32
    )
    grad_key = jnp.einsum(
        "axgcbs,acxgd->bsxd", grad_scores, q_part, preferred_element_type=jnp.float32
    )
    return (grad_query, jnp.stack([grad_key, grad_value]))


def on_device(queries, keys, values, out_grad, order):
    row_count = queries.shape[0]
    block_rows = row_count // 2
    head_width = HEAD_DIM
    score_scale = 1.0 / math.sqrt(head_width)
    cycle_size = lax.axis_size("ctx")
    span_count = 2 * cycle_size
    my_index = lax.axis_index("ctx")
    key_value = jnp.stack([keys, values])
    kv_local = keys.shape[1] // head_width
    q_heads = queries.shape[1] // head_width
    group_size = HEADS // KV_HEADS
    native = key_value.reshape(2, 2, block_rows, kv_local, head_width)
    order_pairs = order.reshape(cycle_size, 2)
    span_low = jnp.min(order_pairs, axis=1)
    low_first = order_pairs[:, 0] < order_pairs[:, 1]
    offsets = jnp.arange(block_rows, dtype=jnp.int32)
    my_low = span_low[my_index]
    my_flag = low_first[my_index]

    def span_positions(low_span):
        return (
            jnp.stack([low_span, span_count - 1 - low_span])[:, None] * block_rows
            + offsets[None, :]
        )

    def sort_kv(blocks, source):
        return jnp.where(low_first[source], blocks, blocks[:, ::-1])

    def store(buffer, blocks, source):
        return lax.dynamic_update_index_in_dim(buffer, blocks, source, 0)

    q_blocks = queries.reshape(2, block_rows, kv_local, group_size, head_width)
    g_blocks = out_grad.reshape(2, block_rows, kv_local, group_size, head_width)
    q_sorted = jnp.where(my_flag, q_blocks, q_blocks[::-1])
    g_sorted = jnp.where(my_flag, g_blocks, g_blocks[::-1])
    q_pos = span_positions(my_low)

    def forward_step(carry_state, kv_sorted, source):
        src_low = span_low[source]
        k_pos = span_positions(src_low)

        def forward_own_case(state_in):
            return attend(state_in, q_sorted, q_pos, kv_sorted[0], kv_sorted[1], k_pos, score_scale)

        def forward_early_case(state_in):
            return attend(
                state_in,
                q_sorted,
                q_pos,
                kv_sorted[0, :1],
                kv_sorted[1, :1],
                k_pos[:1],
                score_scale,
            )

        def forward_late_case(state_in):
            upper_state = attend(
                tuple((member[1:] for member in state_in)),
                q_sorted[1:],
                q_pos[1:],
                kv_sorted[0],
                kv_sorted[1],
                k_pos,
                score_scale,
            )
            return tuple(
                (
                    jnp.concatenate([member[:1], fresh_member], 0)
                    for member, fresh_member in zip(state_in, upper_state)
                )
            )

        branch = jnp.where(source == my_index, 0, jnp.where(src_low < my_low, 1, 2))
        return lax.switch(
            branch, (forward_own_case, forward_early_case, forward_late_case), carry_state
        )

    state_shape = (2, kv_local, group_size, block_rows)
    start_state = (
        jnp.full(state_shape, NEG, jnp.float32),
        jnp.zeros(state_shape, jnp.float32),
        jnp.zeros(state_shape + (head_width,), jnp.float32),
    )
    own_kv = sort_kv(native, my_index)
    kept_blocks = store(jnp.zeros((cycle_size,) + own_kv.shape, jnp.bfloat16), own_kv, my_index)
    fwd_state = forward_step(start_state, own_kv, my_index)

    def cycle_turn(turn_index, loop_carry):
        held, stored, state_now = loop_carry
        held = shifted(held, "ctx", 1)
        source = (my_index - turn_index) % cycle_size
        kv_sorted = sort_kv(held, source)
        return (held, store(stored, kv_sorted, source), forward_step(state_now, kv_sorted, source))

    held_last, kept_blocks, fwd_state = lax.fori_loop(
        1, cycle_size, cycle_turn, (native, kept_blocks, fwd_state)
    )
    row_top, row_total, weighted = fwd_state
    attention_sorted = (weighted / row_total[..., None]).astype(jnp.bfloat16)
    log_total = row_top + jnp.log(row_total)
    grad_heads = g_sorted.transpose(0, 2, 3, 1, 4)
    row_dot = jnp.sum(grad_heads.astype(jnp.float32) * attention_sorted.astype(jnp.float32), axis=4)
    attention_rows = attention_sorted.transpose(0, 3, 1, 2, 4)
    attention_out = jnp.where(my_flag, attention_rows, attention_rows[::-1]).reshape(
        row_count, q_heads * head_width
    )

    def backward_pieces(source):
        kv_sorted = lax.dynamic_index_in_dim(kept_blocks, source, 0, keepdims=False)
        src_low = span_low[source]
        k_pos = span_positions(src_low)

        def backward_own_case():
            return attend_back(
                q_sorted,
                g_sorted,
                log_total,
                row_dot,
                q_pos,
                kv_sorted[0],
                kv_sorted[1],
                k_pos,
                score_scale,
            )

        def backward_early_case():
            query_part, kv_part = attend_back(
                q_sorted,
                g_sorted,
                log_total,
                row_dot,
                q_pos,
                kv_sorted[0, :1],
                kv_sorted[1, :1],
                k_pos[:1],
                score_scale,
            )
            return (query_part, jnp.concatenate([kv_part, jnp.zeros_like(kv_part)], 1))

        def backward_late_case():
            query_part, kv_part = attend_back(
                q_sorted[1:],
                g_sorted[1:],
                log_total[1:],
                row_dot[1:],
                q_pos[1:],
                kv_sorted[0],
                kv_sorted[1],
                k_pos,
                score_scale,
            )
            return (jnp.concatenate([jnp.zeros_like(query_part), query_part], 0), kv_part)

        branch = jnp.where(source == my_index, 0, jnp.where(src_low < my_low, 1, 2))
        return lax.switch(branch, (backward_own_case, backward_early_case, backward_late_case))

    zero_grads = jnp.zeros((2, 2, block_rows, kv_local, head_width), jnp.float32)
    zero_query = jnp.zeros(q_sorted.shape, jnp.float32)

    def grads_turn(turn_index, loop_carry):
        moving, query_sum = loop_carry
        source = (my_index - turn_index) % cycle_size
        query_part, kv_part = backward_pieces(source)
        moving = shifted(moving + kv_part, "ctx", 1)
        return (moving, query_sum + query_part)

    key_grads, query_grads = lax.fori_loop(0, cycle_size, grads_turn, (zero_grads, zero_query))
    key_grads = jnp.where(my_flag, key_grads, key_grads[:, ::-1]).reshape(
        2, row_count, kv_local * head_width
    )
    grad_keys = (score_scale * key_grads[0]).astype(jnp.bfloat16)
    grad_values = key_grads[1].astype(jnp.bfloat16)
    query_rows = jnp.where(my_flag, query_grads, query_grads[::-1]).reshape(
        row_count, q_heads * head_width
    )
    grad_queries = (score_scale * query_rows).astype(jnp.bfloat16)
    return (attention_out, grad_queries, grad_keys, grad_values)


def solution(mesh):
    return jax.shard_map(
        on_device,
        mesh=mesh,
        in_specs=(P("ctx", "head"), P("ctx", "head"), P("ctx", "head"), P("ctx", "head"), P()),
        out_specs=(P("ctx", "head"), P("ctx", "head"), P("ctx", "head"), P("ctx", "head")),
        check_vma=False,
    )
```

profile of v0, /device:TPU:0, one launch (start us, length us, event | category | flops | bytes accessed | tf_op | source)
XLA Modules:
  0.0 320.1 jit_solution(17260328275710323168)
XLA Ops:
  16.4 101.5 %while.42 = (s32[]{:T(128)}, bf16[2,2,80,4,128]{4,2,1,3,0:T(8,128)(2,1)S(1)}, bf16[8,2,2,80,4,128]{5,3,2,4,1,0:T(8,128)(2,1)}, f32[2,4,4,80]{3,2,1,0:T(4,128)S(1...) while((s32[]{:T(128)}, ...), condition=%wide.region_22.23_spmd.clone, body=%wide.region_6.22_spmd.clone.sunk | while | flops 215652192 | bytes 18194028 | solution.py:166
  16.4 3.0 collective-permute-start
  23.3 6.9 %collective-permute-done = bf16[2,2,80,4,128]{4,2,1,3,0:T(8,128)(2,1)S(1)} collective-permute-done((bf16[2,2,80,4,128]{4,2,1,3,0:T(8,128)(2,1)S(1)}, bf16[2,2,80,4,128]{4,2,1,3,0:T(8,128)(2,1)S(1)}, u32[]{:S(2)}, u32[]{:S(2)}) %collective-permute-start) | collective-permute-done | bytes 327712 | tf_op jit(solution)/shard_map/while/body/eval_jaxpr/ppermute | solution.py:18
  37.8 7.7 %collective-permute-done = bf16[2,2,80,4,128]{4,2,1,3,0:T(8,128)(2,1)S(1)} collective-permute-done((bf16[2,2,80,4,128]{4,2,1,3,0:T(8,128)(2,1)S(1)}, bf16[2,2,80,4,128]{4,2,1,3,0:T(8,128)(2,1)S(1)}, u32[]{:S(2)}, u32[]{:S(2)}) %collective-permute-start) | collective-permute-done | bytes 327712 | tf_op jit(solution)/shard_map/while/body/eval_jaxpr/ppermute | solution.py:18
  53.2 6.8 %collective-permute-done = bf16[2,2,80,4,128]{4,2,1,3,0:T(8,128)(2,1)S(1)} collective-permute-done((bf16[2,2,80,4,128]{4,2,1,3,0:T(8,128)(2,1)S(1)}, bf16[2,2,80,4,128]{4,2,1,3,0:T(8,128)(2,1)S(1)}, u32[]{:S(2)}, u32[]{:S(2)}) %collective-permute-start) | collective-permute-done | bytes 327712 | tf_op jit(solution)/shard_map/while/body/eval_jaxpr/ppermute | solution.py:18
  67.6 5.8 %collective-permute-done = bf16[2,2,80,4,128]{4,2,1,3,0:T(8,128)(2,1)S(1)} collective-permute-done((bf16[2,2,80,4,128]{4,2,1,3,0:T(8,128)(2,1)S(1)}, bf16[2,2,80,4,128]{4,2,1,3,0:T(8,128)(2,1)S(1)}, u32[]{:S(2)}, u32[]{:S(2)}) %collective-permute-start) | collective-permute-done | bytes 327712 | tf_op jit(solution)/shard_map/while/body/eval_jaxpr/ppermute | solution.py:18
  81.2 5.8 %collective-permute-done = bf16[2,2,80,4,128]{4,2,1,3,0:T(8,128)(2,1)S(1)} collective-permute-done((bf16[2,2,80,4,128]{4,2,1,3,0:T(8,128)(2,1)S(1)}, bf16[2,2,80,4,128]{4,2,1,3,0:T(8,128)(2,1)S(1)}, u32[]{:S(2)}, u32[]{:S(2)}) %collective-permute-start) | collective-permute-done | bytes 327712 | tf_op jit(solution)/shard_map/while/body/eval_jaxpr/ppermute | solution.py:18
  94.8 5.8 %collective-permute-done = bf16[2,2,80,4,128]{4,2,1,3,0:T(8,128)(2,1)S(1)} collective-permute-done((bf16[2,2,80,4,128]{4,2,1,3,0:T(8,128)(2,1)S(1)}, bf16[2,2,80,4,128]{4,2,1,3,0:T(8,128)(2,1)S(1)}, u32[]{:S(2)}, u32[]{:S(2)}) %collective-permute-start) | collective-permute-done | bytes 327712 | tf_op jit(solution)/shard_map/while/body/eval_jaxpr/ppermute | solution.py:18
  108.4 5.8 %collective-permute-done = bf16[2,2,80,4,128]{4,2,1,3,0:T(8,128)(2,1)S(1)} collective-permute-done((bf16[2,2,80,4,128]{4,2,1,3,0:T(8,128)(2,1)S(1)}, bf16[2,2,80,4,128]{4,2,1,3,0:T(8,128)(2,1)S(1)}, u32[]{:S(2)}, u32[]{:S(2)}) %collective-permute-start) | collective-permute-done | bytes 327712 | tf_op jit(solution)/shard_map/while/body/eval_jaxpr/ppermute | solution.py:18
  120.3 3.0 fusion.119
  124.4 187.1 %while.43 = (s32[]{:T(128)}, f32[2,2,80,4,128]{4,2,1,3,0:T(8,128)}, f32[2,80,4,4,128]{4,1,3,2,0:T(8,128)}, s32[]{:T(128)}, s32[8]{0:T(128)S(1)}, /*index=5*/s32[...) while((s32[]{:T(128)}, f32[2,2,80,4,128]{4,2,1,3,0:T(8,128)}, ...), condition=%wide.region_28.29_spmd.clone, body=%wide.region_24.28_spmd.clone.sunk | while | flops 530212192 | bytes 29793356 | solution.py:238
  128.7 4.3 %conditional.7 = (f32[2,80,4,4,128]{4,1,3,2,0:T(8,128)S(1)}, f32[2,2,80,4,128]{4,2,1,3,0:T(8,128)S(1)}) conditional(s32[]{:T(128)} %clamp.26, (s32[2,80]{1,0:T(2,128)S(1)}, s32[2,80]{1,0:T(2,128)S(1)}, bf16[2,2,80,4,128]{4,2,1,3,0:T(8,128)(2,1)S(1)}, bf16[2,80,4,4,128]{4,1,3,2,0:T(8,128)(2,1)S(1)}, ...), branch_computations={%region_25.25_spmd, %region_26.26_spmd, %region_27.27_spmd} | conditional | flops 529392640 | bytes 17995024 | solution.py:226
  136.2 12.3 %collective-permute-done.1 = f32[2,2,80,4,128]{4,2,1,3,0:T(8,128)S(1)} collective-permute-done((f32[2,2,80,4,128]{4,2,1,3,0:T(8,128)}, f32[2,2,80,4,128]{4,2,1,3,0:T(8,128)S(1)}, u32[]{:S(2)}, u32[]{:S(2)}) %collective-permute-start.1) | collective-permute-done | bytes 655392 | tf_op jit(solution)/shard_map/while/body/eval_jaxpr/ppermute | solution.py:18
  160.5 10.9 %collective-permute-done.1 = f32[2,2,80,4,128]{4,2,1,3,0:T(8,128)S(1)} collective-permute-done((f32[2,2,80,4,128]{4,2,1,3,0:T(8,128)}, f32[2,2,80,4,128]{4,2,1,3,0:T(8,128)S(1)}, u32[]{:S(2)}, u32[]{:S(2)}) %collective-permute-start.1) | collective-permute-done | bytes 655392 | tf_op jit(solution)/shard_map/while/body/eval_jaxpr/ppermute | solution.py:18
  176.5 2.8 conditional.7
  183.9 10.9 %collective-permute-done.1 = f32[2,2,80,4,128]{4,2,1,3,0:T(8,128)S(1)} collective-permute-done((f32[2,2,80,4,128]{4,2,1,3,0:T(8,128)}, f32[2,2,80,4,128]{4,2,1,3,0:T(8,128)S(1)}, u32[]{:S(2)}, u32[]{:S(2)}) %collective-permute-start.1) | collective-permute-done | bytes 655392 | tf_op jit(solution)/shard_map/while/body/eval_jaxpr/ppermute | solution.py:18
  204.3 2.5 select_add_fusion.2
  206.8 10.9 %collective-permute-done.1 = f32[2,2,80,4,128]{4,2,1,3,0:T(8,128)S(1)} collective-permute-done((f32[2,2,80,4,128]{4,2,1,3,0:T(8,128)}, f32[2,2,80,4,128]{4,2,1,3,0:T(8,128)S(1)}, u32[]{:S(2)}, u32[]{:S(2)}) %collective-permute-start.1) | collective-permute-done | bytes 655392 | tf_op jit(solution)/shard_map/while/body/eval_jaxpr/ppermute | solution.py:18
  229.8 10.9 %collective-permute-done.1 = f32[2,2,80,4,128]{4,2,1,3,0:T(8,128)S(1)} collective-permute-done((f32[2,2,80,4,128]{4,2,1,3,0:T(8,128)}, f32[2,2,80,4,128]{4,2,1,3,0:T(8,128)S(1)}, u32[]{:S(2)}, u32[]{:S(2)}) %collective-permute-start.1) | collective-permute-done | bytes 655392 | tf_op jit(solution)/shard_map/while/body/eval_jaxpr/ppermute | solution.py:18
  245.9 2.8 conditional.7
  253.2 10.9 %collective-permute-done.1 = f32[2,2,80,4,128]{4,2,1,3,0:T(8,128)S(1)} collective-permute-done((f32[2,2,80,4,128]{4,2,1,3,0:T(8,128)}, f32[2,2,80,4,128]{4,2,1,3,0:T(8,128)S(1)}, u32[]{:S(2)}, u32[]{:S(2)}) %collective-permute-start.1) | collective-permute-done | bytes 655392 | tf_op jit(solution)/shard_map/while/body/eval_jaxpr/ppermute | solution.py:18
  269.3 2.8 conditional.7
  276.6 11.1 %collective-permute-done.1 = f32[2,2,80,4,128]{4,2,1,3,0:T(8,128)S(1)} collective-permute-done((f32[2,2,80,4,128]{4,2,1,3,0:T(8,128)}, f32[2,2,80,4,128]{4,2,1,3,0:T(8,128)S(1)}, u32[]{:S(2)}, u32[]{:S(2)}) %collective-permute-start.1) | collective-permute-done | bytes 655392 | tf_op jit(solution)/shard_map/while/body/eval_jaxpr/ppermute | solution.py:18
  299.7 10.9 %collective-permute-done.1 = f32[2,2,80,4,128]{4,2,1,3,0:T(8,128)S(1)} collective-permute-done((f32[2,2,80,4,128]{4,2,1,3,0:T(8,128)}, f32[2,2,80,4,128]{4,2,1,3,0:T(8,128)S(1)}, u32[]{:S(2)}, u32[]{:S(2)}) %collective-permute-start.1) | collective-permute-done | bytes 655392 | tf_op jit(solution)/shard_map/while/body/eval_jaxpr/ppermute | solution.py:18
  (331 shorter events, 171.2 us)
Async XLA Ops:
  6.3 3.5 %copy-start.3 = (bf16[160,2048]{1,0:T(8,128)(2,1)S(1)}, bf16[160,2048]{1,0:T(8,128)(2,1)}, u32[]{:S(2)}) copy-start(bf16[160,2048]{1,0:T(8,128)(2,1)} %param.15) | copy-start | bytes 1966084
  16.4 13.8 %collective-permute-start = (bf16[2,2,80,4,128]{4,2,1,3,0:T(8,128)(2,1)S(1)}, bf16[2,2,80,4,128]{4,2,1,3,0:T(8,128)(2,1)S(1)}, u32[]{:S(2)}, u32[]{:S(2)}) collective-permute-start(bf16[2,2,80,4,128]{4,2,1,3,0:T(8,128)(2,1)S(1)} %get-tuple-element.1331), channel_id=1, source_target_pairs={{0,4},{4,8},{8,12},{12,16},{16,20},{20,24},{24,28},{28,0},{1,5},{5... | collective-permute-start | bytes 983048 | tf_op jit(solution)/shard_map/while/body/eval_jaxpr/ppermute | solution.py:18
  33.8 11.6 %collective-permute-start = (bf16[2,2,80,4,128]{4,2,1,3,0:T(8,128)(2,1)S(1)}, bf16[2,2,80,4,128]{4,2,1,3,0:T(8,128)(2,1)S(1)}, u32[]{:S(2)}, u32[]{:S(2)}) collective-permute-start(bf16[2,2,80,4,128]{4,2,1,3,0:T(8,128)(2,1)S(1)} %get-tuple-element.1331), channel_id=1, source_target_pairs={{0,4},{4,8},{8,12},{12,16},{16,20},{20,24},{24,28},{28,0},{1,5},{5... | collective-permute-start | bytes 983048 | tf_op jit(solution)/shard_map/while/body/eval_jaxpr/ppermute | solution.py:18
  49.3 10.7 %collective-permute-start = (bf16[2,2,80,4,128]{4,2,1,3,0:T(8,128)(2,1)S(1)}, bf16[2,2,80,4,128]{4,2,1,3,0:T(8,128)(2,1)S(1)}, u32[]{:S(2)}, u32[]{:S(2)}) collective-permute-start(bf16[2,2,80,4,128]{4,2,1,3,0:T(8,128)(2,1)S(1)} %get-tuple-element.1331), channel_id=1, source_target_pairs={{0,4},{4,8},{8,12},{12,16},{16,20},{20,24},{24,28},{28,0},{1,5},{5... | collective-permute-start | bytes 983048 | tf_op jit(solution)/shard_map/while/body/eval_jaxpr/ppermute | solution.py:18
  63.7 9.8 %collective-permute-start = (bf16[2,2,80,4,128]{4,2,1,3,0:T(8,128)(2,1)S(1)}, bf16[2,2,80,4,128]{4,2,1,3,0:T(8,128)(2,1)S(1)}, u32[]{:S(2)}, u32[]{:S(2)}) collective-permute-start(bf16[2,2,80,4,128]{4,2,1,3,0:T(8,128)(2,1)S(1)} %get-tuple-element.1331), channel_id=1, source_target_pairs={{0,4},{4,8},{8,12},{12,16},{16,20},{20,24},{24,28},{28,0},{1,5},{5... | collective-permute-start | bytes 983048 | tf_op jit(solution)/shard_map/while/body/eval_jaxpr/ppermute | solution.py:18
  77.2 9.8 %collective-permute-start = (bf16[2,2,80,4,128]{4,2,1,3,0:T(8,128)(2,1)S(1)}, bf16[2,2,80,4,128]{4,2,1,3,0:T(8,128)(2,1)S(1)}, u32[]{:S(2)}, u32[]{:S(2)}) collective-permute-start(bf16[2,2,80,4,128]{4,2,1,3,0:T(8,128)(2,1)S(1)} %get-tuple-element.1331), channel_id=1, source_target_pairs={{0,4},{4,8},{8,12},{12,16},{16,20},{20,24},{24,28},{28,0},{1,5},{5... | collective-permute-start | bytes 983048 | tf_op jit(solution)/shard_map/while/body/eval_jaxpr/ppermute | solution.py:18
  90.8 9.8 %collective-permute-start = (bf16[2,2,80,4,128]{4,2,1,3,0:T(8,128)(2,1)S(1)}, bf16[2,2,80,4,128]{4,2,1,3,0:T(8,128)(2,1)S(1)}, u32[]{:S(2)}, u32[]{:S(2)}) collective-permute-start(bf16[2,2,80,4,128]{4,2,1,3,0:T(8,128)(2,1)S(1)} %get-tuple-element.1331), channel_id=1, source_target_pairs={{0,4},{4,8},{8,12},{12,16},{16,20},{20,24},{24,28},{28,0},{1,5},{5... | collective-permute-start | bytes 983048 | tf_op jit(solution)/shard_map/while/body/eval_jaxpr/ppermute | solution.py:18
  104.4 9.8 %collective-permute-start = (bf16[2,2,80,4,128]{4,2,1,3,0:T(8,128)(2,1)S(1)}, bf16[2,2,80,4,128]{4,2,1,3,0:T(8,128)(2,1)S(1)}, u32[]{:S(2)}, u32[]{:S(2)}) collective-permute-start(bf16[2,2,80,4,128]{4,2,1,3,0:T(8,128)(2,1)S(1)} %get-tuple-element.1331), channel_id=1, source_target_pairs={{0,4},{4,8},{8,12},{12,16},{16,20},{20,24},{24,28},{28,0},{1,5},{5... | collective-permute-start | bytes 983048 | tf_op jit(solution)/shard_map/while/body/eval_jaxpr/ppermute | solution.py:18
  135.0 13.5 %collective-permute-start.1 = (f32[2,2,80,4,128]{4,2,1,3,0:T(8,128)}, f32[2,2,80,4,128]{4,2,1,3,0:T(8,128)S(1)}, u32[]{:S(2)}, u32[]{:S(2)}) collective-permute-start(f32[2,2,80,4,128]{4,2,1,3,0:T(8,128)} %add.366), channel_id=1, source_target_pairs={{0,4},{4,8},{8,12},{12,16},{16,20},{20,24},{24,28},{28,0},{1,5},{5... | collective-permute-start | bytes 1966088 | tf_op jit(solution)/shard_map/while/body/eval_jaxpr/ppermute | solution.py:18
  148.5 0.8 copy-start.1
  157.9 13.5 %collective-permute-start.1 = (f32[2,2,80,4,128]{4,2,1,3,0:T(8,128)}, f32[2,2,80,4,128]{4,2,1,3,0:T(8,128)S(1)}, u32[]{:S(2)}, u32[]{:S(2)}) collective-permute-start(f32[2,2,80,4,128]{4,2,1,3,0:T(8,128)} %add.366), channel_id=1, source_target_pairs={{0,4},{4,8},{8,12},{12,16},{16,20},{20,24},{24,28},{28,0},{1,5},{5... | collective-permute-start | bytes 1966088 | tf_op jit(solution)/shard_map/while/body/eval_jaxpr/ppermute | solution.py:18
  171.4 0.8 copy-start.1
  181.3 13.5 %collective-permute-start.1 = (f32[2,2,80,4,128]{4,2,1,3,0:T(8,128)}, f32[2,2,80,4,128]{4,2,1,3,0:T(8,128)S(1)}, u32[]{:S(2)}, u32[]{:S(2)}) collective-permute-start(f32[2,2,80,4,128]{4,2,1,3,0:T(8,128)} %add.366), channel_id=1, source_target_pairs={{0,4},{4,8},{8,12},{12,16},{16,20},{20,24},{24,28},{28,0},{1,5},{5... | collective-permute-start | bytes 1966088 | tf_op jit(solution)/shard_map/while/body/eval_jaxpr/ppermute | solution.py:18
  194.8 0.8 copy-start.1
  204.3 13.5 %collective-permute-start.1 = (f32[2,2,80,4,128]{4,2,1,3,0:T(8,128)}, f32[2,2,80,4,128]{4,2,1,3,0:T(8,128)S(1)}, u32[]{:S(2)}, u32[]{:S(2)}) collective-permute-start(f32[2,2,80,4,128]{4,2,1,3,0:T(8,128)} %add.366), channel_id=1, source_target_pairs={{0,4},{4,8},{8,12},{12,16},{16,20},{20,24},{24,28},{28,0},{1,5},{5... | collective-permute-start | bytes 1966088 | tf_op jit(solution)/shard_map/while/body/eval_jaxpr/ppermute | solution.py:18
  227.2 13.5 %collective-permute-start.1 = (f32[2,2,80,4,128]{4,2,1,3,0:T(8,128)}, f32[2,2,80,4,128]{4,2,1,3,0:T(8,128)S(1)}, u32[]{:S(2)}, u32[]{:S(2)}) collective-permute-start(f32[2,2,80,4,128]{4,2,1,3,0:T(8,128)} %add.366), channel_id=1, source_target_pairs={{0,4},{4,8},{8,12},{12,16},{16,20},{20,24},{24,28},{28,0},{1,5},{5... | collective-permute-start | bytes 1966088 | tf_op jit(solution)/shard_map/while/body/eval_jaxpr/ppermute | solution.py:18
  240.7 0.8 copy-start.1
  250.7 13.5 %collective-permute-start.1 = (f32[2,2,80,4,128]{4,2,1,3,0:T(8,128)}, f32[2,2,80,4,128]{4,2,1,3,0:T(8,128)S(1)}, u32[]{:S(2)}, u32[]{:S(2)}) collective-permute-start(f32[2,2,80,4,128]{4,2,1,3,0:T(8,128)} %add.366), channel_id=1, source_target_pairs={{0,4},{4,8},{8,12},{12,16},{16,20},{20,24},{24,28},{28,0},{1,5},{5... | collective-permute-start | bytes 1966088 | tf_op jit(solution)/shard_map/while/body/eval_jaxpr/ppermute | solution.py:18
  274.1 13.6 %collective-permute-start.1 = (f32[2,2,80,4,128]{4,2,1,3,0:T(8,128)}, f32[2,2,80,4,128]{4,2,1,3,0:T(8,128)S(1)}, u32[]{:S(2)}, u32[]{:S(2)}) collective-permute-start(f32[2,2,80,4,128]{4,2,1,3,0:T(8,128)} %add.366), channel_id=1, source_target_pairs={{0,4},{4,8},{8,12},{12,16},{16,20},{20,24},{24,28},{28,0},{1,5},{5... | collective-permute-start | bytes 1966088 | tf_op jit(solution)/shard_map/while/body/eval_jaxpr/ppermute | solution.py:18
  287.7 0.8 copy-start.1
  297.2 13.5 %collective-permute-start.1 = (f32[2,2,80,4,128]{4,2,1,3,0:T(8,128)}, f32[2,2,80,4,128]{4,2,1,3,0:T(8,128)S(1)}, u32[]{:S(2)}, u32[]{:S(2)}) collective-permute-start(f32[2,2,80,4,128]{4,2,1,3,0:T(8,128)} %add.366), channel_id=1, source_target_pairs={{0,4},{4,8},{8,12},{12,16},{16,20},{20,24},{24,28},{28,0},{1,5},{5... | collective-permute-start | bytes 1966088 | tf_op jit(solution)/shard_map/while/body/eval_jaxpr/ppermute | solution.py:18
  310.7 0.8 copy-start.1
  313.5 1.4 copy-start
  315.4 2.4 copy-start.2
  (2 other events, 1.7 us)
where the time goes:
time: 323 us; the launch traced here: 320 us
  waiting for transfers between devices  134 us (41%)
  other arithmetic  75.9 us (23%)
  local copies, waits for them, and re-layouts  43.9 us (14%)
  matrix products  31.7 us (10%)
  loops' own time  29.9 us (9%)
  starting transfers between devices  3.41 us (1%)
    ppermute x15, waiting for transfers between devices, shifted(): lax.ppermute(array, axis, [(i, (i + by) % length) for i in range(length)])  134 us
    add x8, other arithmetic, grads_turn(): return (moving, query_sum + query_part)  19 us
    add x8, other arithmetic, grads_turn(): moving = shifted(moving + kv_part, 'ctx', 1)  16 us
    another operation x1, loops' own time, on_device(): lax.fori_loop(0, cycle_size, grads_turn, (zero_grads, zero_query))  15.3 us
    another operation x1, loops' own time, on_device(): lax.fori_loop(1, cycle_size, cycle_turn, (native, kept_blocks, fwd_state))  13.8 us
    dynamic_update_slice x8, other arithmetic, store(): return lax.dynamic_update_index_in_dim(buffer, blocks, source, 0)  11.7 us
    mul x16, other arithmetic, span_positions(): jnp.stack([low_span, span_count - 1 - low_span])[:, None] * block_rows  11.4 us
    squeeze x8, local copies, waits for them, and re-layouts, backward_pieces(): kv_sorted = lax.dynamic_index_in_dim(kept_blocks, source, 0, keepdims=False)  7.95 us
  transfers between devices with their start and end apart: 15, of which 15 were waited for; matrix products, arithmetic and copies ran while one was open for 10% of the time, Pallas kernels for 0%

commit v1 on v0

v1 whole, which is shorter than its diff:
```python
import functools
import math

import jax
import jax.numpy as jnp
from jax import lax
from jax.experimental import pallas as pl
from jax.experimental.pallas import tpu as pltpu
from jax.sharding import PartitionSpec as P

HEADS = 32
KV_HEADS = 8
HEAD_DIM = 128
GROUP = HEADS // KV_HEADS
NEG = -1e30
MESH = pl.DeviceIdType.MESH

UP, DOWN = 0, 1


def line_lengths(n_ctx):
    n0 = 4 if n_ctx % 4 == 0 else 1
    return n0, n_ctx // n0


def dot_nt(a, b):
    return lax.dot_general(a, b, (((1,), (1,)), ((), ())), preferred_element_type=jnp.float32)


def dot_tn(a, b):
    return lax.dot_general(a, b, (((0,), (0,)), ((), ())), preferred_element_type=jnp.float32)


def dot_nn(a, b):
    return lax.dot_general(a, b, (((1,), (0,)), ((), ())), preferred_element_type=jnp.float32)


def kernel(
    n_ctx, kv_heads, rows, chunk, kinds,
    q_ref, k_ref, v_ref, g_ref, order_ref,
    att_ref, dq_ref, dk_ref, dv_ref,
    kv, bias, probs, qs, gs, att_t, dq_t, acc,
    send_s, recv_s, send_f, recv_f,
    ag_send, ag_recv, s_send, s_recv, f_send, f_recv,
):
    n0, n1 = line_lengths(n_ctx)
    me = lax.axis_index("ctx")
    i0, i1 = me // n1, me % n1
    span = rows // 2
    keys_all = n_ctx * rows
    q_rows = GROUP * rows
    scale = 1.0 / math.sqrt(HEAD_DIM)
    to_exp2 = scale * math.log2(math.e)

    class Kind:
        def __init__(self, index):
            self.index = index
            first_is_0 = kinds[index] == 0
            self.nf, self.ns = (n0, n1) if first_is_0 else (n1, n0)
            self.f, self.s = (i0, i1) if first_is_0 else (i1, i0)
            self.first_is_0 = first_is_0

        def device(self, f, s):
            return f * n1 + s if self.first_is_0 else s * n1 + f

        def slot(self, f, s):
            return s * self.nf + f

        def neighbour(self, line, direction):
            step = 1 if direction == UP else -1
            if line == 0:
                return self.device(self.f + step, self.s)
            return self.device(self.f, self.s + step)

        def has(self, line, direction):
            x, n = (self.f, self.nf) if line == 0 else (self.s, self.ns)
            return x + 1 < n if direction == UP else x > 0

    kind_list = [Kind(i) for i in range(len(kinds))]

    def kind_of(h):
        return kind_list[h % len(kinds)]

    def block(slot):
        return pl.ds(pl.multiple_of(slot * rows, rows), rows)

    barrier = pltpu.get_barrier_semaphore()
    base = kind_list[0]
    for line in (0, 1):
        for direction in (UP, DOWN):
            @pl.when(base.has(line, direction))
            def _(line=line, direction=direction):
                pl.semaphore_signal(
                    barrier, inc=1, device_id={"ctx": base.neighbour(line, direction)},
                    device_id_type=MESH,
                )
    peers = sum(
        base.has(line, direction).astype(jnp.int32) for line in (0, 1) for direction in (UP, DOWN)
    )
    pl.semaphore_wait(barrier, peers)

    def ag_copy(h, slot, line, direction):
        kind = kind_of(h)
        return pltpu.make_async_remote_copy(
            src_ref=kv.at[h, block(slot)],
            dst_ref=kv.at[h, block(slot)],
            send_sem=ag_send.at[h, slot, 2 * line + direction],
            recv_sem=ag_recv.at[h, slot],
            device_id={"ctx": kind.neighbour(line, direction)},
            device_id_type=MESH,
        )

    def ag_stage(h, stage, op):
        kind = kind_of(h)
        nf, ns, f, s = kind.nf, kind.ns, kind.f, kind.s

        def push(slot, line, direction):
            @pl.when(kind.has(line, direction))
            def _():
                copy = ag_copy(h, slot, line, direction)
                if op == "go":
                    copy.start()
                else:
                    copy.wait_send()

        def arrived(slot):
            if op == "go":
                ag_copy(h, slot, 0, UP).wait_recv()

        if stage == 0:
            own = kind.slot(f, s)
            if op == "go":
                columns = pl.ds(h * HEAD_DIM, HEAD_DIM)
                kv[h, block(own), 0:HEAD_DIM] = k_ref[:, columns]
                kv[h, block(own), HEAD_DIM:] = v_ref[:, columns]
            for line in (0, 1):
                push(own, line, UP)
                push(own, line, DOWN)
        elif stage < nf:
            for origin, direction in ((f - stage, UP), (f + stage, DOWN)):
                @pl.when(jnp.logical_and(origin >= 0, origin < nf))
                def _(origin=origin, direction=direction):
                    slot = kind.slot(origin, s)
                    arrived(slot)
                    push(slot, 0, direction)
                    push(slot, 1, UP)
                    push(slot, 1, DOWN)
        else:
            d = stage - nf + 1
            for origin, direction in ((s - d, UP), (s + d, DOWN)):
                @pl.when(jnp.logical_and(origin >= 0, origin < ns))
                def _(origin=origin, direction=direction):
                    for from_f in range(nf):
                        slot = kind.slot(from_f, origin)
                        arrived(slot)
                        push(slot, 1, direction)

    def ag_stages(h):
        return kind_of(h).nf + kind_of(h).ns - 1

    def line_copy(h, line, x, direction):
        kind = kind_of(h)
        if line == 1:
            size = kind.nf * rows
            where = pl.ds(pl.multiple_of(x * size, size), size)
            src, dst, sends, recvs = send_s, recv_s, s_send, s_recv
        else:
            where = block(x)
            src, dst, sends, recvs = send_f, recv_f, f_send, f_recv
        return pltpu.make_async_remote_copy(
            src_ref=src.at[h, where],
            dst_ref=dst.at[h, direction, where],
            send_sem=sends.at[h, x],
            recv_sem=recvs.at[h, direction, x],
            device_id={"ctx": kind.neighbour(line, direction)},
            device_id_type=MESH,
        )

    def acc_rows(h, line, x):
        kind = kind_of(h)
        if line == 1:
            size = kind.nf * rows
            return pl.ds(pl.multiple_of(x * size, size), size)
        return block(kind.slot(x, kind.s))

    def line_rows(h, line, x):
        kind = kind_of(h)
        size = kind.nf * rows if line == 1 else rows
        return pl.ds(pl.multiple_of(x * size, size), size)

    def chain_stage(h, line, stage, op):
        kind = kind_of(h)
        at, n = (kind.f, kind.nf) if line == 0 else (kind.s, kind.ns)
        src, dst = (send_f, recv_f) if line == 0 else (send_s, recv_s)

        def pass_on(x, direction):
            copy = line_copy(h, line, x, direction)
            if op == "sent":
                copy.wait_send()
                return
            total = acc[h, acc_rows(h, line, x)]
            if stage > 0:
                copy.wait_recv()
                total = total + dst[h, direction, line_rows(h, line, x)].astype(jnp.float32)
            src[h, line_rows(h, line, x)] = total.astype(jnp.bfloat16)
            copy.start()

        @pl.when(at == stage)
        def _():
            for x in range(n - 1, stage, -1):
                pass_on(x, UP)

        @pl.when(at == n - 1 - stage)
        def _():
            for x in range(0, n - 1 - stage):
                pass_on(x, DOWN)

    def chain_end(h, line):
        kind = kind_of(h)
        at, n = (kind.f, kind.nf) if line == 0 else (kind.s, kind.ns)
        dst = recv_f if line == 0 else recv_s
        for direction, there in ((UP, at > 0), (DOWN, at < n - 1)):
            @pl.when(there)
            def _(direction=direction):
                line_copy(h, line, at, direction).wait_recv()
                where = acc_rows(h, line, at)
                acc[h, where] = acc[h, where] + dst[
                    h, direction, line_rows(h, line, at)
                ].astype(jnp.float32)

    def write_kv_grads(h):
        kind = kind_of(h)
        where = block(kind.slot(kind.f, kind.s))
        columns = pl.ds(h * HEAD_DIM, HEAD_DIM)
        dk_ref[:, columns] = (acc[h, where, 0:HEAD_DIM] * scale).astype(jnp.bfloat16)
        dv_ref[:, columns] = acc[h, where, HEAD_DIM:].astype(jnp.bfloat16)

    def rs_tasks(h):
        kind = kind_of(h)
        tasks = []
        for stage in range(1, kind.ns - 1):
            tasks.append(functools.partial(chain_stage, h, 1, stage, "go"))

        def turn():
            chain_end(h, 1)
            chain_stage(h, 0, 0, "go")

        tasks.append(turn)
        for stage in range(1, kind.nf - 1):
            tasks.append(functools.partial(chain_stage, h, 0, stage, "go"))

        def finish():
            chain_end(h, 0)
            write_kv_grads(h)

        tasks.append(finish)
        return tasks

    def make_bias(kind):
        lane = lax.broadcasted_iota(jnp.int32, (1, q_rows), 1) % rows
        low, high = order_ref[2 * me], order_ref[2 * me + 1]
        q_pos = jnp.where(lane < span, low * span + lane, high * span + lane - span)
        row = lax.broadcasted_iota(jnp.int32, (span, q_rows), 0)

        @pl.loop(0, n_ctx)
        def _(slot):
            source = kind.device(slot % kind.nf, slot // kind.nf)
            for half in range(2):
                k_pos = row + order_ref[2 * source + half] * span
                where = pl.ds(pl.multiple_of(slot * rows + half * span, span), span)
                bias[kind.index, where] = jnp.where(k_pos <= q_pos, 0.0, NEG)

    def load_queries(h):
        for g in range(GROUP):
            columns = pl.ds((h * GROUP + g) * HEAD_DIM, HEAD_DIM)
            qs[pl.ds(g * rows, rows)] = q_ref[:, columns]
            gs[pl.ds(g * rows, rows)] = g_ref[:, columns]

    def rows_of(i):
        return pl.ds(pl.multiple_of(i * chunk, chunk), chunk)

    def fold(x, op):
        return op(x.reshape(chunk // 8, 8, q_rows), axis=0)

    def scores_pass(h):
        kind = kind_of(h)

        def body(i, top):
            where = rows_of(i)
            s = dot_nt(kv[h, where, 0:HEAD_DIM], qs[...]) + bias[kind.index, where]
            probs[where] = s
            return jnp.maximum(top, fold(s, jnp.max))

        top = lax.fori_loop(
            0, keys_all // chunk, body, jnp.full((8, q_rows), NEG, jnp.float32)
        )
        return jnp.max(top, axis=0, keepdims=True) * to_exp2

    def weights_pass(h, top):
        att_t[...] = jnp.zeros_like(att_t)

        def body(i, total):
            where = rows_of(i)
            e = jnp.exp2(probs[where] * to_exp2 - top)
            probs[where] = e
            att_t[...] += dot_tn(kv[h, where, HEAD_DIM:], e.astype(jnp.bfloat16))
            return total + fold(e, jnp.sum)

        total = lax.fori_loop(
            0, keys_all // chunk, body, jnp.zeros((8, q_rows), jnp.float32)
        )
        inverse = 1.0 / jnp.sum(total, axis=0, keepdims=True)
        attention = (att_t[...] * inverse).T.astype(jnp.bfloat16)
        for g in range(GROUP):
            columns = pl.ds((h * GROUP + g) * HEAD_DIM, HEAD_DIM)
            att_ref[:, columns] = attention[g * rows:(g + 1) * rows]
        product = gs[...].astype(jnp.float32) * attention.astype(jnp.float32)
        row_dot = jnp.sum(product.T, axis=0, keepdims=True)
        return inverse, row_dot

    def backward_group(h, s, inverse, row_dot):
        kind = kind_of(h)
        per_group = kind.nf * rows // chunk

        @pl.loop(0, per_group)
        def _(j):
            where = rows_of(s * per_group + j)
            k, v = kv[h, where, 0:HEAD_DIM], kv[h, where, HEAD_DIM:]
            p = probs[where] * inverse
            ds = (p * (dot_nt(v, gs[...]) - row_dot)).astype(jnp.bfloat16)
            acc[h, where, 0:HEAD_DIM] = dot_nn(ds, qs[...])
            acc[h, where, HEAD_DIM:] = dot_nn(p.astype(jnp.bfloat16), gs[...])
            dq_t[...] += dot_tn(k, ds)

    def write_dq(h):
        dq = (dq_t[...] * scale).T.astype(jnp.bfloat16)
        for g in range(GROUP):
            columns = pl.ds((h * GROUP + g) * HEAD_DIM, HEAD_DIM)
            dq_ref[:, columns] = dq[g * rows:(g + 1) * rows]

    lag = 2
    ticks = []
    last_tick = lag * (kv_heads - 1) + max(ag_stages(h) for h in range(kv_heads))
    for t in range(last_tick):
        ticks.append([
            (h, t - lag * h) for h in range(kv_heads) if 0 <= t - lag * h < ag_stages(h)
        ])
    done = 0

    def run_ticks(until):
        nonlocal done
        while done < min(until, len(ticks)):
            for h, stage in ticks[done]:
                ag_stage(h, stage, "go")
            done += 1

    pending = []

    def run_pending(count):
        for _ in range(min(count, len(pending))):
            pending.pop(0)()

    run_ticks(1)
    for kind in kind_list:
        make_bias(kind)
    load_queries(0)
    for h in range(kv_heads):
        kind = kind_of(h)
        run_ticks(lag * h + ag_stages(h))
        if h:
            load_queries(h)
        top = scores_pass(h)
        run_ticks(lag * h + ag_stages(h) + 1)
        run_pending(1)
        inverse, row_dot = weights_pass(h, top)
        run_ticks(lag * h + ag_stages(h) + 2)
        run_pending(1)
        dq_t[...] = jnp.zeros_like(dq_t)

        def away(j, _):
            backward_group(h, lax.rem(kind.s + j, kind.ns), inverse, row_dot)
            return 0

        lax.fori_loop(1, kind.ns, away, 0)
        run_pending(1)
        chain_stage(h, 1, 0, "go")
        backward_group(h, kind.s, inverse, row_dot)
        run_pending(len(pending))
        write_dq(h)
        pending.extend(rs_tasks(h))
    run_pending(len(pending))

    for h in range(kv_heads):
        for stage in range(ag_stages(h)):
            ag_stage(h, stage, "sent")
        for line in (1, 0):
            kind = kind_of(h)
            for stage in range((kind.ns if line else kind.nf) - 1):
                chain_stage(h, line, stage, "sent")


def on_device(n_ctx, queries, keys, values, out_grad, order):
    rows = queries.shape[0]
    kv_heads = keys.shape[1] // HEAD_DIM
    q_rows = GROUP * rows
    keys_all = n_ctx * rows
    n0, n1 = line_lengths(n_ctx)
    kinds = (0, 1) if kv_heads > 1 else (0,)
    wide = 2 * HEAD_DIM
    longest = max(n0, n1)
    chunk = 2 * rows
    vmem = pl.BlockSpec(memory_space=pltpu.VMEM)
    return pl.pallas_call(
        functools.partial(kernel, n_ctx, kv_heads, rows, chunk, kinds),
        out_shape=[
            jax.ShapeDtypeStruct(x.shape, jnp.bfloat16) for x in (queries, queries, keys, values)
        ],
        in_specs=[vmem] * 4 + [pl.BlockSpec(memory_space=pltpu.SMEM)],
        out_specs=[vmem] * 4,
        scratch_shapes=[
            pltpu.VMEM((kv_heads, keys_all, wide), jnp.bfloat16),
            pltpu.VMEM((len(kinds), keys_all, q_rows), jnp.float32),
            pltpu.VMEM((keys_all, q_rows), jnp.float32),
            pltpu.VMEM((q_rows, HEAD_DIM), jnp.bfloat16),
            pltpu.VMEM((q_rows, HEAD_DIM), jnp.bfloat16),
            pltpu.VMEM((HEAD_DIM, q_rows), jnp.float32),
            pltpu.VMEM((HEAD_DIM, q_rows), jnp.float32),
            pltpu.VMEM((kv_heads, keys_all, wide), jnp.float32),
            pltpu.VMEM((kv_heads, keys_all, wide), jnp.bfloat16),
            pltpu.VMEM((kv_heads, 2, keys_all, wide), jnp.bfloat16),
            pltpu.VMEM((kv_heads, longest * rows, wide), jnp.bfloat16),
            pltpu.VMEM((kv_heads, 2, longest * rows, wide), jnp.bfloat16),
            pltpu.SemaphoreType.DMA((kv_heads, n_ctx, 4)),
            pltpu.SemaphoreType.DMA((kv_heads, n_ctx)),
            pltpu.SemaphoreType.DMA((kv_heads, longest)),
            pltpu.SemaphoreType.DMA((kv_heads, 2, longest)),
            pltpu.SemaphoreType.DMA((kv_heads, longest)),
            pltpu.SemaphoreType.DMA((kv_heads, 2, longest)),
        ],
        compiler_params=pltpu.CompilerParams(
            collective_id=0, has_side_effects=True, vmem_limit_bytes=60 * 1024 * 1024
        ),
        name="attention_fwd_bwd",
    )(queries, keys, values, out_grad, order)


def solution(mesh):
    return jax.shard_map(
        functools.partial(on_device, mesh.shape["ctx"]),
        mesh=mesh,
        in_specs=(P("ctx", "head"), P("ctx", "head"), P("ctx", "head"), P("ctx", "head"), P()),
        out_specs=(P("ctx", "head"), P("ctx", "head"), P("ctx", "head"), P("ctx", "head")),
        check_vma=False,
    )
```

time: 323 us -> 98.8 us (0.31)
  waiting for transfers between devices: 134 us -> 0 us
  Pallas kernels: 0 us -> 93.2 us
  other arithmetic: 75.9 us -> 0 us
  local copies, waits for them, and re-layouts: 43.9 us -> 4.75 us
  matrix products: 31.7 us -> 0 us
  loops' own time: 29.9 us -> 0 us
  starting transfers between devices: 3.41 us -> 0 us
    ppermute x15 -> x0, waiting for transfers between devices: 134 us -> none  [shifted(): lax.ppermute(array, axis, [(i, (i + by) % length) for i in range(length)])]
    pallas_call x0 -> x1, Pallas kernels: none -> 93.2 us  [on_device(): pl.pallas_call(functools.partial(kernel, n_ctx, kv_heads, rows, chunk, ki...]
    add x37 -> x0, other arithmetic: 36.7 us -> none  [the longest x8 19 us: grads_turn(): return (moving, query_sum + query_part)]
    dot_general x56 -> x0, matrix products: 31.7 us -> none  [the longest x8 7.37 us: attend(): jnp.einsum('axgcbs,bsxd->axgcbd', block_weights.astype(jnp.bfloat16), v_p...]
    another operation x17 -> x0, loops' own time: 29.9 us -> none  [the longest x1 15.3 us: on_device(): lax.fori_loop(0, cycle_size, grads_turn, (zero_grads, zero_query))]
    dynamic_slice x24 -> x0, local copies, waits for them, and re-layouts: 14.2 us -> none  [the longest x8 4.89 us: backward_pieces(): src_low = span_low[source]]
    dynamic_update_slice x8 -> x0, other arithmetic: 11.7 us -> none  [store(): return lax.dynamic_update_index_in_dim(buffer, blocks, source, 0)]
    mul x20 -> x0, other arithmetic: 11.4 us -> none  [the longest x16 11.4 us: span_positions(): jnp.stack([low_span, span_count - 1 - low_span])[:, None] * block_rows]
  transfers between devices with their start and end apart: 15 -> 0, of which waited for: 15 -> 0; matrix products, arithmetic and copies ran while one was open for 10% -> 0% of each run, Pallas kernels for 0% -> 0%
where the time goes in v1:
time: 98.8 us; the launch traced here: 98.6 us
  Pallas kernels  93.2 us (94%)
  local copies, waits for them, and re-layouts  4.75 us (5%)
    pallas_call x1, Pallas kernels, on_device(): pl.pallas_call(functools.partial(kernel, n_ctx, kv_heads, rows, chunk, ki...  93.2 us
    unnamed x10, local copies, waits for them, and re-layouts  4.75 us

profile of v1, /device:TPU:0, one launch (start us, length us, event | category | flops | bytes accessed | tf_op | source)
XLA Modules:
  0.0 98.6 jit_solution(2484451299050840461)
XLA Ops:
  0.6 93.2 %attention_fwd_bwd.1 = (bf16[160,2048]{1,0:T(8,128)(2,1)}, bf16[160,2048]{1,0:T(8,128)(2,1)}, bf16[160,512]{1,0:T(8,128)(2,1)}, bf16[160,512]{1,0:T(8,128)(2,1)}) custom-call(bf16[160,2048]{1,0:T(8,128)(2,1)} %q_ref.1, bf16[160,512]{1,0:T(8,128)(2,1)} %k_ref.1, bf16[160,512]{1,0:T(8,128)(2,1)} %v_ref.1, bf16[160,2048]{1,0:T(8,128)(2,1)} %g_ref.1, s32[16]{0:T(128)} %order_ref.1), custom_call_target="tpu_custom_call" | custom-call | tf_op jit(solution)/shard_map/attention_fwd_bwd/pallas_call | solution.py:413
  93.8 0.0 copy-start
  93.8 2.0 %copy.13 = bf16[160,2048]{1,0:T(8,128)(2,1)} copy(bf16[160,2048]{1,0:T(8,128)(2,1)} %get-tuple-element.8) | data formatting | bytes 1310720
  95.9 0.0 copy-done
  95.9 0.0 copy-start.2
  95.9 0.8 copy.14
  96.7 0.2 copy-done.2
  96.9 0.0 copy-start.1
  96.9 0.7 copy.15
  97.6 0.3 copy-done.1
  97.9 0.7 copy.16
Async XLA Ops:
  93.8 2.1 %copy-start = (bf16[160,2048]{1,0:T(8,128)(2,1)S(1)}, bf16[160,2048]{1,0:T(8,128)(2,1)}, u32[]{:S(2)}) copy-start(bf16[160,2048]{1,0:T(8,128)(2,1)} %get-tuple-element.9) | copy-start | bytes 1966084
  95.9 1.1 %copy-start.2 = (bf16[160,512]{1,0:T(8,128)(2,1)S(1)}, bf16[160,512]{1,0:T(8,128)(2,1)}, u32[]{:S(2)}) copy-start(bf16[160,512]{1,0:T(8,128)(2,1)} %get-tuple-element.10) | copy-start | bytes 491524
  96.9 1.0 copy-start.1

commit v2 on v1

--- a/solution.py
+++ b/solution.py
@@ -79,7 +79,7 @@
     kind_list = [Kind(i) for i in range(len(kinds))]
 
     def kind_of(h):
-        return kind_list[h % len(kinds)]
+        return kind_list[1 if h % 4 == 1 else 0]
 
     def block(slot):
         return pl.ds(pl.multiple_of(slot * rows, rows), rows)
@@ -158,103 +158,108 @@
     def ag_stages(h):
         return kind_of(h).nf + kind_of(h).ns - 1
 
-    def line_copy(h, line, x, direction):
-        kind = kind_of(h)
-        if line == 1:
-            size = kind.nf * rows
-            where = pl.ds(pl.multiple_of(x * size, size), size)
-            src, dst, sends, recvs = send_s, recv_s, s_send, s_recv
-        else:
-            where = block(x)
-            src, dst, sends, recvs = send_f, recv_f, f_send, f_recv
+    def s_copy(h, slot, direction):
+        kind = kind_of(h)
         return pltpu.make_async_remote_copy(
-            src_ref=src.at[h, where],
-            dst_ref=dst.at[h, direction, where],
-            send_sem=sends.at[h, x],
-            recv_sem=recvs.at[h, direction, x],
-            device_id={"ctx": kind.neighbour(line, direction)},
+            src_ref=send_s.at[h, block(slot)],
+            dst_ref=recv_s.at[h, direction, block(slot)],
+            send_sem=s_send.at[h, slot],
+            recv_sem=s_recv.at[h, direction, slot],
+            device_id={"ctx": kind.device(kind.f, kind.s + 1 - 2 * direction)},
             device_id_type=MESH,
         )
 
-    def acc_rows(h, line, x):
-        kind = kind_of(h)
-        if line == 1:
-            size = kind.nf * rows
-            return pl.ds(pl.multiple_of(x * size, size), size)
-        return block(kind.slot(x, kind.s))
-
-    def line_rows(h, line, x):
-        kind = kind_of(h)
-        size = kind.nf * rows if line == 1 else rows
-        return pl.ds(pl.multiple_of(x * size, size), size)
-
-    def chain_stage(h, line, stage, op):
-        kind = kind_of(h)
-        at, n = (kind.f, kind.nf) if line == 0 else (kind.s, kind.ns)
-        src, dst = (send_f, recv_f) if line == 0 else (send_s, recv_s)
+    def f_copy(h, x, direction):
+        kind = kind_of(h)
+        return pltpu.make_async_remote_copy(
+            src_ref=send_f.at[h, block(x)],
+            dst_ref=recv_f.at[h, direction, block(x)],
+            send_sem=f_send.at[h, x],
+            recv_sem=f_recv.at[h, direction, x],
+            device_id={"ctx": kind.neighbour(0, direction)},
+            device_id_type=MESH,
+        )
+
+    def s_pass_on(h, slot, direction, first):
+        total = acc[h, block(slot)]
+        copy = s_copy(h, slot, direction)
+        if not first:
+            copy.wait_recv()
+            total = total + recv_s[h, direction, block(slot)].astype(jnp.float32)
+        send_s[h, block(slot)] = total.astype(jnp.bfloat16)
+        copy.start()
+
+    def s_stage(h, stage):
+        kind = kind_of(h)
+        n = kind.ns
+
+        @pl.when(kind.s == stage)
+        def _():
+            for x in range(n - 1, stage, -1):
+                for f in range(kind.nf):
+                    s_pass_on(h, kind.slot(f, x), UP, False)
+
+        @pl.when(kind.s == n - 1 - stage)
+        def _():
+            for x in range(0, n - 1 - stage):
+                for f in range(kind.nf):
+                    s_pass_on(h, kind.slot(f, x), DOWN, False)
+
+    def take_s(h, slot):
+        kind = kind_of(h)
+        for direction, there in ((UP, kind.s > 0), (DOWN, kind.s < kind.ns - 1)):
+            @pl.when(there)
+            def _(direction=direction):
+                s_copy(h, slot, direction).wait_recv()
+                where = block(slot)
+                acc[h, where] = acc[h, where] + recv_s[h, direction, where].astype(jnp.float32)
+
+    def f_stage(h, stage):
+        kind = kind_of(h)
+        n = kind.nf
 
         def pass_on(x, direction):
-            copy = line_copy(h, line, x, direction)
-            if op == "sent":
-                copy.wait_send()
-                return
-            total = acc[h, acc_rows(h, line, x)]
+            slot = kind.slot(x, kind.s)
+            take_s(h, slot)
+            total = acc[h, block(slot)]
+            copy = f_copy(h, x, direction)
             if stage > 0:
                 copy.wait_recv()
-                total = total + dst[h, direction, line_rows(h, line, x)].astype(jnp.float32)
-            src[h, line_rows(h, line, x)] = total.astype(jnp.bfloat16)
+                total = total + recv_f[h, direction, block(x)].astype(jnp.float32)
+            send_f[h, block(x)] = total.astype(jnp.bfloat16)
             copy.start()
 
-        @pl.when(at == stage)
+        @pl.when(kind.f == stage)
         def _():
             for x in range(n - 1, stage, -1):
                 pass_on(x, UP)
 
-        @pl.when(at == n - 1 - stage)
+        @pl.when(kind.f == n - 1 - stage)
         def _():
             for x in range(0, n - 1 - stage):
                 pass_on(x, DOWN)
 
-    def chain_end(h, line):
-        kind = kind_of(h)
-        at, n = (kind.f, kind.nf) if line == 0 else (kind.s, kind.ns)
-        dst = recv_f if line == 0 else recv_s
-        for direction, there in ((UP, at > 0), (DOWN, at < n - 1)):
+    def finish(h):
+        kind = kind_of(h)
+        own = kind.slot(kind.f, kind.s)
+        take_s(h, own)
+        where = block(own)
+        for direction, there in ((UP, kind.f > 0), (DOWN, kind.f < kind.nf - 1)):
             @pl.when(there)
             def _(direction=direction):
-                line_copy(h, line, at, direction).wait_recv()
-                where = acc_rows(h, line, at)
-                acc[h, where] = acc[h, where] + dst[
-                    h, direction, line_rows(h, line, at)
+                f_copy(h, kind.f, direction).wait_recv()
+                acc[h, where] = acc[h, where] + recv_f[
+                    h, direction, block(kind.f)
                 ].astype(jnp.float32)
-
-    def write_kv_grads(h):
-        kind = kind_of(h)
-        where = block(kind.slot(kind.f, kind.s))
         columns = pl.ds(h * HEAD_DIM, HEAD_DIM)
         dk_ref[:, columns] = (acc[h, where, 0:HEAD_DIM] * scale).astype(jnp.bfloat16)
         dv_ref[:, columns] = acc[h, where, HEAD_DIM:].astype(jnp.bfloat16)
 
     def rs_tasks(h):
         kind = kind_of(h)
-        tasks = []
-        for stage in range(1, kind.ns - 1):
-            tasks.append(functools.partial(chain_stage, h, 1, stage, "go"))
-
-        def turn():
-            chain_end(h, 1)
-            chain_stage(h, 0, 0, "go")
-
-        tasks.append(turn)
-        for stage in range(1, kind.nf - 1):
-            tasks.append(functools.partial(chain_stage, h, 0, stage, "go"))
-
-        def finish():
-            chain_end(h, 0)
-            write_kv_grads(h)
-
-        tasks.append(finish)
-        return tasks
+        tasks = [functools.partial(s_stage, h, stage) for stage in range(1, kind.ns - 1)]
+        tasks += [functools.partial(f_stage, h, stage) for stage in range(kind.nf - 1)]
+        return tasks + [functools.partial(finish, h)]
 
     def make_bias(kind):
         lane = lax.broadcasted_iota(jnp.int32, (1, q_rows), 1) % rows
@@ -276,23 +281,25 @@
             qs[pl.ds(g * rows, rows)] = q_ref[:, columns]
             gs[pl.ds(g * rows, rows)] = g_ref[:, columns]
 
-    def rows_of(i):
-        return pl.ds(pl.multiple_of(i * chunk, chunk), chunk)
+    def rows_of(i, size):
+        return pl.ds(pl.multiple_of(i * size, size), size)
+
+    tall = 2 * chunk
 
     def fold(x, op):
-        return op(x.reshape(chunk // 8, 8, q_rows), axis=0)
+        return op(x.reshape(tall // 8, 8, q_rows), axis=0)
 
     def scores_pass(h):
         kind = kind_of(h)
 
         def body(i, top):
-            where = rows_of(i)
+            where = rows_of(i, tall)
             s = dot_nt(kv[h, where, 0:HEAD_DIM], qs[...]) + bias[kind.index, where]
             probs[where] = s
             return jnp.maximum(top, fold(s, jnp.max))
 
         top = lax.fori_loop(
-            0, keys_all // chunk, body, jnp.full((8, q_rows), NEG, jnp.float32)
+            0, keys_all // tall, body, jnp.full((8, q_rows), NEG, jnp.float32)
         )
         return jnp.max(top, axis=0, keepdims=True) * to_exp2
 
@@ -300,14 +307,14 @@
         att_t[...] = jnp.zeros_like(att_t)
 
         def body(i, total):
-            where = rows_of(i)
+            where = rows_of(i, tall)
             e = jnp.exp2(probs[where] * to_exp2 - top)
             probs[where] = e
             att_t[...] += dot_tn(kv[h, where, HEAD_DIM:], e.astype(jnp.bfloat16))
             return total + fold(e, jnp.sum)
 
         total = lax.fori_loop(
-            0, keys_all // chunk, body, jnp.zeros((8, q_rows), jnp.float32)
+            0, keys_all // tall, body, jnp.zeros((8, q_rows), jnp.float32)
         )
         inverse = 1.0 / jnp.sum(total, axis=0, keepdims=True)
         attention = (att_t[...] * inverse).T.astype(jnp.bfloat16)
@@ -318,19 +325,35 @@
         row_dot = jnp.sum(product.T, axis=0, keepdims=True)
         return inverse, row_dot
 
-    def backward_group(h, s, inverse, row_dot):
+    def backward_group(h, s, inverse, row_dot, send):
         kind = kind_of(h)
         per_group = kind.nf * rows // chunk
-
-        @pl.loop(0, per_group)
-        def _(j):
-            where = rows_of(s * per_group + j)
+        direction = jnp.where(s > kind.s, UP, DOWN)
+        first = jnp.logical_or(
+            jnp.logical_and(s > kind.s, kind.s == 0),
+            jnp.logical_and(s < kind.s, kind.s == kind.ns - 1),
+        )
+        backwards = kind.f < kind.nf // 2
+
+        def body(j, _):
+            j = jnp.where(backwards, per_group - 1 - j, j)
+            where = rows_of(s * per_group + j, chunk)
             k, v = kv[h, where, 0:HEAD_DIM], kv[h, where, HEAD_DIM:]
             p = probs[where] * inverse
             ds = (p * (dot_nt(v, gs[...]) - row_dot)).astype(jnp.bfloat16)
             acc[h, where, 0:HEAD_DIM] = dot_nn(ds, qs[...])
             acc[h, where, HEAD_DIM:] = dot_nn(p.astype(jnp.bfloat16), gs[...])
             dq_t[...] += dot_tn(k, ds)
+            if send:
+                @pl.when(first)
+                def _():
+                    per_chunk = chunk // rows
+                    for b in range(per_chunk):
+                        b = jnp.where(backwards, per_chunk - 1 - b, b)
+                        s_pass_on(h, (s * per_group + j) * per_chunk + b, direction, True)
+            return 0
+
+        lax.fori_loop(0, per_group, body, 0)
 
     def write_dq(h):
         dq = (dq_t[...] * scale).T.astype(jnp.bfloat16)
@@ -354,11 +377,13 @@
                 ag_stage(h, stage, "go")
             done += 1
 
-    pending = []
-
-    def run_pending(count):
-        for _ in range(min(count, len(pending))):
-            pending.pop(0)()
+    chains = []
+
+    def advance():
+        for chain in list(chains):
+            chain.pop(0)()
+            if not chain:
+                chains.remove(chain)
 
     run_ticks(1)
     for kind in kind_list:
@@ -371,32 +396,63 @@
             load_queries(h)
         top = scores_pass(h)
         run_ticks(lag * h + ag_stages(h) + 1)
-        run_pending(1)
         inverse, row_dot = weights_pass(h, top)
         run_ticks(lag * h + ag_stages(h) + 2)
-        run_pending(1)
+        advance()
         dq_t[...] = jnp.zeros_like(dq_t)
 
         def away(j, _):
-            backward_group(h, lax.rem(kind.s + j, kind.ns), inverse, row_dot)
+            backward_group(h, lax.rem(kind.s + j, kind.ns), inverse, row_dot, True)
             return 0
 
         lax.fori_loop(1, kind.ns, away, 0)
-        run_pending(1)
-        chain_stage(h, 1, 0, "go")
-        backward_group(h, kind.s, inverse, row_dot)
-        run_pending(len(pending))
+        backward_group(h, kind.s, inverse, row_dot, False)
+        advance()
+        chains.append(rs_tasks(h))
+        if h == kv_heads - 1:
+            advance()
         write_dq(h)
-        pending.extend(rs_tasks(h))
-    run_pending(len(pending))
+    while chains:
+        advance()
 
     for h in range(kv_heads):
+        kind = kind_of(h)
         for stage in range(ag_stages(h)):
             ag_stage(h, stage, "sent")
-        for line in (1, 0):
-            kind = kind_of(h)
-            for stage in range((kind.ns if line else kind.nf) - 1):
-                chain_stage(h, line, stage, "sent")
+
+        def sent(j, _):
+            group = lax.rem(kind.s + j, kind.ns)
+            for f in range(kind.nf):
+                s_copy(h, kind.slot(f, group), UP).wait_send()
+            return 0
+
+        lax.fori_loop(1, kind.ns, sent, 0)
+        for j in range(1, kind.nf):
+            f_copy(h, lax.rem(kind.f + j, kind.nf), UP).wait_send()
+
+
+def copy_kernel(*refs):
+    sems = refs[-1]
+    count = (len(refs) - 1) // 2
+    copies = [
+        pltpu.make_async_copy(refs[i], refs[count + i], sems.at[i]) for i in range(count)
+    ]
+    for copy in copies:
+        copy.start()
+    for copy in copies:
+        copy.wait()
+
+
+def hand_out(results):
+    anywhere = pl.BlockSpec(memory_space=pl.ANY)
+    return pl.pallas_call(
+        copy_kernel,
+        out_shape=[jax.ShapeDtypeStruct(x.shape, x.dtype) for x in results],
+        in_specs=[anywhere] * len(results),
+        out_specs=[anywhere] * len(results),
+        scratch_shapes=[pltpu.SemaphoreType.DMA((len(results),))],
+        name="hand_out",
+    )(*results)
 
 
 def on_device(n_ctx, queries, keys, values, out_grad, order):
@@ -410,7 +466,7 @@
     longest = max(n0, n1)
     chunk = 2 * rows
     vmem = pl.BlockSpec(memory_space=pltpu.VMEM)
-    return pl.pallas_call(
+    results = pl.pallas_call(
         functools.partial(kernel, n_ctx, kv_heads, rows, chunk, kinds),
         out_shape=[
             jax.ShapeDtypeStruct(x.shape, jnp.bfloat16) for x in (queries, queries, keys, values)
@@ -432,8 +488,8 @@
             pltpu.VMEM((kv_heads, 2, longest * rows, wide), jnp.bfloat16),
             pltpu.SemaphoreType.DMA((kv_heads, n_ctx, 4)),
             pltpu.SemaphoreType.DMA((kv_heads, n_ctx)),
-            pltpu.SemaphoreType.DMA((kv_heads, longest)),
-            pltpu.SemaphoreType.DMA((kv_heads, 2, longest)),
+            pltpu.SemaphoreType.DMA((kv_heads, n_ctx)),
+            pltpu.SemaphoreType.DMA((kv_heads, 2, n_ctx)),
             pltpu.SemaphoreType.DMA((kv_heads, longest)),
             pltpu.SemaphoreType.DMA((kv_heads, 2, longest)),
         ],
@@ -442,6 +498,7 @@
         ),
         name="attention_fwd_bwd",
     )(queries, keys, values, out_grad, order)
+    return tuple(hand_out(results))
 
 
 def solution(mesh):

time: 98.8 us -> 134 us (1.36)
  Pallas kernels: 93.2 us -> 133 us
  local copies, waits for them, and re-layouts: 4.75 us -> 0 us
    pallas_call x0 -> x1, Pallas kernels: none -> 50.8 us  [hand_out(): pl.pallas_call(copy_kernel, out_shape=[jax.ShapeDtypeStruct(x.shape, x.dt...]
    pallas_call x1, Pallas kernels: 93.2 us -> 82.7 us  [on_device(): pl.pallas_call(functools.partial(kernel, n_ctx, kv_heads, rows, chunk, ki...]
    unnamed x10 -> x0, local copies, waits for them, and re-layouts: 4.75 us -> none
where the time goes in v2:
time: 134 us
  Pallas kernels  133 us (99%)
    pallas_call x1, Pallas kernels, on_device(): pl.pallas_call(functools.partial(kernel, n_ctx, kv_heads, rows, chunk, ki...  82.7 us
    pallas_call x1, Pallas kernels, hand_out(): pl.pallas_call(copy_kernel, out_shape=[jax.ShapeDtypeStruct(x.shape, x.dt...  50.8 us

profile of v2, /device:TPU:0, one launch (start us, length us, event | category | flops | bytes accessed | tf_op | source)
XLA Modules:
  0.0 134.1 jit_solution(8979614609613559991)
XLA Ops:
  0.6 82.7 %attention_fwd_bwd.1 = (bf16[160,2048]{1,0:T(8,128)(2,1)}, bf16[160,2048]{1,0:T(8,128)(2,1)}, bf16[160,512]{1,0:T(8,128)(2,1)}, bf16[160,512]{1,0:T(8,128)(2,1)}) custom-call(bf16[160,2048]{1,0:T(8,128)(2,1)} %q_ref.1, bf16[160,512]{1,0:T(8,128)(2,1)} %k_ref.1, bf16[160,512]{1,0:T(8,128)(2,1)} %v_ref.1, bf16[160,2048]{1,0:T(8,128)(2,1)} %g_ref.1, s32[16]{0:T(128)} %order_ref.1), custom_call_target="tpu_custom_call" | custom-call | tf_op jit(solution)/shard_map/attention_fwd_bwd/pallas_call | solution.py:469
  83.3 50.8 %hand_out.1 = (bf16[160,2048]{1,0:T(8,128)(2,1)}, bf16[160,2048]{1,0:T(8,128)(2,1)}, bf16[160,512]{1,0:T(8,128)(2,1)}, bf16[160,512]{1,0:T(8,128)(2,1)}) custom-call(bf16[160,2048]{1,0:T(8,128)(2,1)} %get-tuple-element.8.refs_0_, bf16[160,2048]{1,0:T(8,128)(2,1)} %get-tuple-element.9.refs_1_, bf16[160,512]{1,0:T(8,128)(2,1)} %get-tuple-element.10.refs_2_, ...), custom_call_target="tpu_custom_call" | custom-call | tf_op jit(solution)/shard_map/hand_out/pallas_call | solution.py:448

commit v3 on v2

--- a/solution.py
+++ b/solution.py
@@ -36,7 +36,7 @@
 
 
 def kernel(
-    n_ctx, kv_heads, rows, chunk, kinds,
+    n_ctx, kv_heads, rows, kinds,
     q_ref, k_ref, v_ref, g_ref, order_ref,
     att_ref, dq_ref, dk_ref, dv_ref,
     kv, bias, probs, qs, gs, att_t, dq_t, acc,
@@ -47,8 +47,9 @@
     me = lax.axis_index("ctx")
     i0, i1 = me // n1, me % n1
     span = rows // 2
-    keys_all = n_ctx * rows
+    half_keys = n_ctx * span
     q_rows = GROUP * rows
+    skip = q_rows // 2 // 128 * 128
     scale = 1.0 / math.sqrt(HEAD_DIM)
     to_exp2 = scale * math.log2(math.e)
 
@@ -82,7 +83,13 @@
         return kind_list[1 if h % 4 == 1 else 0]
 
     def block(slot):
-        return pl.ds(pl.multiple_of(slot * rows, rows), rows)
+        return pl.ds(pl.multiple_of(slot * span, span), span)
+
+    first_span, second_span = order_ref[2 * me], order_ref[2 * me + 1]
+    low_first = first_span < second_span
+
+    def sort_halves(a, b):
+        return jnp.where(low_first, a, b), jnp.where(low_first, b, a)
 
     barrier = pltpu.get_barrier_semaphore()
     base = kind_list[0]
@@ -102,8 +109,8 @@
     def ag_copy(h, slot, line, direction):
         kind = kind_of(h)
         return pltpu.make_async_remote_copy(
-            src_ref=kv.at[h, block(slot)],
-            dst_ref=kv.at[h, block(slot)],
+            src_ref=kv.at[h, :, block(slot)],
+            dst_ref=kv.at[h, :, block(slot)],
             send_sem=ag_send.at[h, slot, 2 * line + direction],
             recv_sem=ag_recv.at[h, slot],
             device_id={"ctx": kind.neighbour(line, direction)},
@@ -131,8 +138,10 @@
             own = kind.slot(f, s)
             if op == "go":
                 columns = pl.ds(h * HEAD_DIM, HEAD_DIM)
-                kv[h, block(own), 0:HEAD_DIM] = k_ref[:, columns]
-                kv[h, block(own), HEAD_DIM:] = v_ref[:, columns]
+                for ref, lanes in ((k_ref, pl.ds(0, HEAD_DIM)), (v_ref, pl.ds(HEAD_DIM, HEAD_DIM))):
+                    low, high = sort_halves(ref[0:span, columns], ref[span:, columns])
+                    kv[h, 0, block(own), lanes] = low
+                    kv[h, 1, block(own), lanes] = high
             for line in (0, 1):
                 push(own, line, UP)
                 push(own, line, DOWN)
@@ -161,8 +170,8 @@
     def s_copy(h, slot, direction):
         kind = kind_of(h)
         return pltpu.make_async_remote_copy(
-            src_ref=send_s.at[h, block(slot)],
-            dst_ref=recv_s.at[h, direction, block(slot)],
+            src_ref=send_s.at[h, :, block(slot)],
+            dst_ref=recv_s.at[h, direction, :, block(slot)],
             send_sem=s_send.at[h, slot],
             recv_sem=s_recv.at[h, direction, slot],
             device_id={"ctx": kind.device(kind.f, kind.s + 1 - 2 * direction)},
@@ -172,8 +181,8 @@
     def f_copy(h, x, direction):
         kind = kind_of(h)
         return pltpu.make_async_remote_copy(
-            src_ref=send_f.at[h, block(x)],
-            dst_ref=recv_f.at[h, direction, block(x)],
+            src_ref=send_f.at[h, :, block(x)],
+            dst_ref=recv_f.at[h, direction, :, block(x)],
             send_sem=f_send.at[h, x],
             recv_sem=f_recv.at[h, direction, x],
             device_id={"ctx": kind.neighbour(0, direction)},
@@ -181,12 +190,12 @@
         )
 
     def s_pass_on(h, slot, direction, first):
-        total = acc[h, block(slot)]
+        total = acc[h, :, block(slot)]
         copy = s_copy(h, slot, direction)
         if not first:
             copy.wait_recv()
-            total = total + recv_s[h, direction, block(slot)].astype(jnp.float32)
-        send_s[h, block(slot)] = total.astype(jnp.bfloat16)
+            total = total + recv_s[h, direction, :, block(slot)].astype(jnp.float32)
+        send_s[h, :, block(slot)] = total.astype(jnp.bfloat16)
         copy.start()
 
     def s_stage(h, stage):
@@ -212,7 +221,7 @@
             def _(direction=direction):
                 s_copy(h, slot, direction).wait_recv()
                 where = block(slot)
-                acc[h, where] = acc[h, where] + recv_s[h, direction, where].astype(jnp.float32)
+                acc[h, :, where] = acc[h, :, where] + recv_s[h, direction, :, where].astype(jnp.float32)
 
     def f_stage(h, stage):
         kind = kind_of(h)
@@ -221,12 +230,12 @@
         def pass_on(x, direction):
             slot = kind.slot(x, kind.s)
             take_s(h, slot)
-            total = acc[h, block(slot)]
+            total = acc[h, :, block(slot)]
             copy = f_copy(h, x, direction)
             if stage > 0:
                 copy.wait_recv()
-                total = total + recv_f[h, direction, block(x)].astype(jnp.float32)
-            send_f[h, block(x)] = total.astype(jnp.bfloat16)
+                total = total + recv_f[h, direction, :, block(x)].astype(jnp.float32)
+            send_f[h, :, block(x)] = total.astype(jnp.bfloat16)
             copy.start()
 
         @pl.when(kind.f == stage)
@@ -248,12 +257,15 @@
             @pl.when(there)
             def _(direction=direction):
                 f_copy(h, kind.f, direction).wait_recv()
-                acc[h, where] = acc[h, where] + recv_f[
-                    h, direction, block(kind.f)
+                acc[h, :, where] = acc[h, :, where] + recv_f[
+                    h, direction, :, block(kind.f)
                 ].astype(jnp.float32)
         columns = pl.ds(h * HEAD_DIM, HEAD_DIM)
-        dk_ref[:, columns] = (acc[h, where, 0:HEAD_DIM] * scale).astype(jnp.bfloat16)
-        dv_ref[:, columns] = acc[h, where, HEAD_DIM:].astype(jnp.bfloat16)
+        both = sort_halves(acc[h, 0, where], acc[h, 1, where])
+        for i in range(2):
+            rows_here = pl.ds(i * span, span)
+            dk_ref[rows_here, columns] = (both[i][:, :HEAD_DIM] * scale).astype(jnp.bfloat16)
+            dv_ref[rows_here, columns] = both[i][:, HEAD_DIM:].astype(jnp.bfloat16)
 
     def rs_tasks(h):
         kind = kind_of(h)
@@ -262,104 +274,122 @@
         return tasks + [functools.partial(finish, h)]
 
     def make_bias(kind):
-        lane = lax.broadcasted_iota(jnp.int32, (1, q_rows), 1) % rows
-        low, high = order_ref[2 * me], order_ref[2 * me + 1]
-        q_pos = jnp.where(lane < span, low * span + lane, high * span + lane - span)
+        lane = lax.broadcasted_iota(jnp.int32, (1, q_rows), 1)
+        low = jnp.minimum(first_span, second_span) * span
+        high = jnp.maximum(first_span, second_span) * span
+        q_pos = lane % span + jnp.where(lane < GROUP * span, low, high)
         row = lax.broadcasted_iota(jnp.int32, (span, q_rows), 0)
 
         @pl.loop(0, n_ctx)
         def _(slot):
             source = kind.device(slot % kind.nf, slot // kind.nf)
-            for half in range(2):
-                k_pos = row + order_ref[2 * source + half] * span
-                where = pl.ds(pl.multiple_of(slot * rows + half * span, span), span)
-                bias[kind.index, where] = jnp.where(k_pos <= q_pos, 0.0, NEG)
+            a, b = order_ref[2 * source], order_ref[2 * source + 1]
+            for half, start in ((0, jnp.minimum(a, b)), (1, jnp.maximum(a, b))):
+                visible = row + start * span <= q_pos
+                bias[kind.index, half, block(slot)] = jnp.where(visible, 0.0, NEG)
+
+    halves = ((0, 0), (1, skip))
 
     def load_queries(h):
         for g in range(GROUP):
             columns = pl.ds((h * GROUP + g) * HEAD_DIM, HEAD_DIM)
-            qs[pl.ds(g * rows, rows)] = q_ref[:, columns]
-            gs[pl.ds(g * rows, rows)] = g_ref[:, columns]
+            for ref, to in ((q_ref, qs), (g_ref, gs)):
+                low, high = sort_halves(ref[0:span, columns], ref[span:, columns])
+                to[pl.ds(g * span, span)] = low
+                to[pl.ds((GROUP + g) * span, span)] = high
+
+    def write_rows(ref, h, result):
+        for g in range(GROUP):
+            columns = pl.ds((h * GROUP + g) * HEAD_DIM, HEAD_DIM)
+            first, second = sort_halves(
+                result[g * span:(g + 1) * span],
+                result[(GROUP + g) * span:(GROUP + g + 1) * span],
+            )
+            ref[0:span, columns] = first
+            ref[span:, columns] = second
 
     def rows_of(i, size):
         return pl.ds(pl.multiple_of(i * size, size), size)
 
-    tall = 2 * chunk
+    tall = min(half_keys, 4 * span)
 
     def fold(x, op):
-        return op(x.reshape(tall // 8, 8, q_rows), axis=0)
+        return op(x.reshape(x.shape[0] // 8, 8, x.shape[1]), axis=0)
+
+    def join(parts, op):
+        low, high = (op(x, axis=0, keepdims=True) for x in parts)
+        both = op(jnp.concatenate([low[:, skip:], high], axis=0), axis=0, keepdims=True)
+        return jnp.concatenate([low[:, :skip], both], axis=1)
 
     def scores_pass(h):
         kind = kind_of(h)
 
-        def body(i, top):
+        def body(i, tops):
             where = rows_of(i, tall)
-            s = dot_nt(kv[h, where, 0:HEAD_DIM], qs[...]) + bias[kind.index, where]
-            probs[where] = s
-            return jnp.maximum(top, fold(s, jnp.max))
-
-        top = lax.fori_loop(
-            0, keys_all // tall, body, jnp.full((8, q_rows), NEG, jnp.float32)
+            out = []
+            for half, lanes in halves:
+                s = dot_nt(kv[h, half, where, 0:HEAD_DIM], qs[lanes:])
+                s = s + bias[kind.index, half, where, lanes:]
+                probs[half, where, lanes:] = s
+                out.append(jnp.maximum(tops[half], fold(s, jnp.max)))
+            return tuple(out)
+
+        tops = lax.fori_loop(
+            0, half_keys // tall, body,
+            tuple(jnp.full((8, q_rows - lanes), NEG, jnp.float32) for _, lanes in halves),
         )
-        return jnp.max(top, axis=0, keepdims=True) * to_exp2
+        return join(tops, jnp.max) * to_exp2
 
     def weights_pass(h, top):
         att_t[...] = jnp.zeros_like(att_t)
 
-        def body(i, total):
+        def body(i, totals):
             where = rows_of(i, tall)
-            e = jnp.exp2(probs[where] * to_exp2 - top)
-            probs[where] = e
-            att_t[...] += dot_tn(kv[h, where, HEAD_DIM:], e.astype(jnp.bfloat16))
-            return total + fold(e, jnp.sum)
-
-        total = lax.fori_loop(
-            0, keys_all // tall, body, jnp.zeros((8, q_rows), jnp.float32)
+            out = []
+            for half, lanes in halves:
+                e = jnp.exp2(probs[half, where, lanes:] * to_exp2 - top[:, lanes:])
+                probs[half, where, lanes:] = e
+                att_t[:, lanes:] += dot_tn(kv[h, half, where, HEAD_DIM:], e.astype(jnp.bfloat16))
+                out.append(totals[half] + fold(e, jnp.sum))
+            return tuple(out)
+
+        totals = lax.fori_loop(
+            0, half_keys // tall, body,
+            tuple(jnp.zeros((8, q_rows - lanes), jnp.float32) for _, lanes in halves),
         )
-        inverse = 1.0 / jnp.sum(total, axis=0, keepdims=True)
+        inverse = 1.0 / join(totals, jnp.sum)
         attention = (att_t[...] * inverse).T.astype(jnp.bfloat16)
-        for g in range(GROUP):
-            columns = pl.ds((h * GROUP + g) * HEAD_DIM, HEAD_DIM)
-            att_ref[:, columns] = attention[g * rows:(g + 1) * rows]
+        write_rows(att_ref, h, attention)
         product = gs[...].astype(jnp.float32) * attention.astype(jnp.float32)
         row_dot = jnp.sum(product.T, axis=0, keepdims=True)
         return inverse, row_dot
 
     def backward_group(h, s, inverse, row_dot, send):
         kind = kind_of(h)
-        per_group = kind.nf * rows // chunk
-        direction = jnp.where(s > kind.s, UP, DOWN)
-        first = jnp.logical_or(
-            jnp.logical_and(s > kind.s, kind.s == 0),
-            jnp.logical_and(s < kind.s, kind.s == kind.ns - 1),
-        )
-        backwards = kind.f < kind.nf // 2
-
-        def body(j, _):
-            j = jnp.where(backwards, per_group - 1 - j, j)
-            where = rows_of(s * per_group + j, chunk)
-            k, v = kv[h, where, 0:HEAD_DIM], kv[h, where, HEAD_DIM:]
-            p = probs[where] * inverse
-            ds = (p * (dot_nt(v, gs[...]) - row_dot)).astype(jnp.bfloat16)
-            acc[h, where, 0:HEAD_DIM] = dot_nn(ds, qs[...])
-            acc[h, where, HEAD_DIM:] = dot_nn(p.astype(jnp.bfloat16), gs[...])
-            dq_t[...] += dot_tn(k, ds)
-            if send:
-                @pl.when(first)
-                def _():
-                    per_chunk = chunk // rows
-                    for b in range(per_chunk):
-                        b = jnp.where(backwards, per_chunk - 1 - b, b)
-                        s_pass_on(h, (s * per_group + j) * per_chunk + b, direction, True)
-            return 0
-
-        lax.fori_loop(0, per_group, body, 0)
+        where = rows_of(s, kind.nf * span)
+        for half, lanes in halves:
+            k, v = kv[h, half, where, 0:HEAD_DIM], kv[h, half, where, HEAD_DIM:]
+            p = probs[half, where, lanes:] * inverse[:, lanes:]
+            ds = (p * (dot_nt(v, gs[lanes:]) - row_dot[:, lanes:])).astype(jnp.bfloat16)
+            acc[h, half, where, 0:HEAD_DIM] = dot_nn(ds, qs[lanes:])
+            acc[h, half, where, HEAD_DIM:] = dot_nn(p.astype(jnp.bfloat16), gs[lanes:])
+            dq_t[:, lanes:] += dot_tn(k, ds)
+        if send:
+            direction = jnp.where(s > kind.s, UP, DOWN)
+            first = jnp.logical_or(
+                jnp.logical_and(s > kind.s, kind.s == 0),
+                jnp.logical_and(s < kind.s, kind.s == kind.ns - 1),
+            )
+            backwards = kind.f < kind.nf // 2
+
+            @pl.when(first)
+            def _():
+                for b in range(kind.nf):
+                    b = jnp.where(backwards, kind.nf - 1 - b, b)
+                    s_pass_on(h, s * kind.nf + b, direction, True)
 
     def write_dq(h):
-        dq = (dq_t[...] * scale).T.astype(jnp.bfloat16)
-        for g in range(GROUP):
-            columns = pl.ds((h * GROUP + g) * HEAD_DIM, HEAD_DIM)
-            dq_ref[:, columns] = dq[g * rows:(g + 1) * rows]
+        write_rows(dq_ref, h, (dq_t[...] * scale).T.astype(jnp.bfloat16))
 
     lag = 2
     ticks = []
@@ -448,7 +478,7 @@
     return pl.pallas_call(
         copy_kernel,
         out_shape=[jax.ShapeDtypeStruct(x.shape, x.dtype) for x in results],
-        in_specs=[anywhere] * len(results),
+        in_specs=[pl.BlockSpec(memory_space=pltpu.VMEM)] * len(results),
         out_specs=[anywhere] * len(results),
         scratch_shapes=[pltpu.SemaphoreType.DMA((len(results),))],
         name="hand_out",
@@ -459,33 +489,32 @@
     rows = queries.shape[0]
     kv_heads = keys.shape[1] // HEAD_DIM
     q_rows = GROUP * rows
-    keys_all = n_ctx * rows
+    half_keys = n_ctx * rows // 2
     n0, n1 = line_lengths(n_ctx)
     kinds = (0, 1) if kv_heads > 1 else (0,)
     wide = 2 * HEAD_DIM
     longest = max(n0, n1)
-    chunk = 2 * rows
     vmem = pl.BlockSpec(memory_space=pltpu.VMEM)
     results = pl.pallas_call(
-        functools.partial(kernel, n_ctx, kv_heads, rows, chunk, kinds),
+        functools.partial(kernel, n_ctx, kv_heads, rows, kinds),
         out_shape=[
             jax.ShapeDtypeStruct(x.shape, jnp.bfloat16) for x in (queries, queries, keys, values)
         ],
         in_specs=[vmem] * 4 + [pl.BlockSpec(memory_space=pltpu.SMEM)],
         out_specs=[vmem] * 4,
         scratch_shapes=[
-            pltpu.VMEM((kv_heads, keys_all, wide), jnp.bfloat16),
-            pltpu.VMEM((len(kinds), keys_all, q_rows), jnp.float32),
-            pltpu.VMEM((keys_all, q_rows), jnp.float32),
+            pltpu.VMEM((kv_heads, 2, half_keys, wide), jnp.bfloat16),
+            pltpu.VMEM((len(kinds), 2, half_keys, q_rows), jnp.float32),
+            pltpu.VMEM((2, half_keys, q_rows), jnp.float32),
             pltpu.VMEM((q_rows, HEAD_DIM), jnp.bfloat16),
             pltpu.VMEM((q_rows, HEAD_DIM), jnp.bfloat16),
             pltpu.VMEM((HEAD_DIM, q_rows), jnp.float32),
             pltpu.VMEM((HEAD_DIM, q_rows), jnp.float32),
-            pltpu.VMEM((kv_heads, keys_all, wide), jnp.float32),
-            pltpu.VMEM((kv_heads, keys_all, wide), jnp.bfloat16),
-            pltpu.VMEM((kv_heads, 2, keys_all, wide), jnp.bfloat16),
-            pltpu.VMEM((kv_heads, longest * rows, wide), jnp.bfloat16),
-            pltpu.VMEM((kv_heads, 2, longest * rows, wide), jnp.bfloat16),
+            pltpu.VMEM((kv_heads, 2, half_keys, wide), jnp.float32),
+            pltpu.VMEM((kv_heads, 2, half_keys, wide), jnp.bfloat16),
+            pltpu.VMEM((kv_heads, 2, 2, half_keys, wide), jnp.bfloat16),
+            pltpu.VMEM((kv_heads, 2, longest * rows // 2, wide), jnp.bfloat16),
+            pltpu.VMEM((kv_heads, 2, 2, longest * rows // 2, wide), jnp.bfloat16),
             pltpu.SemaphoreType.DMA((kv_heads, n_ctx, 4)),
             pltpu.SemaphoreType.DMA((kv_heads, n_ctx)),
             pltpu.SemaphoreType.DMA((kv_heads, n_ctx)),

time: 134 us -> 86.2 us (0.64)
  Pallas kernels: 133 us -> 85.2 us
    pallas_call x1, Pallas kernels: 50.8 us -> 2.55 us  [hand_out(): pl.pallas_call(copy_kernel, out_shape=[jax.ShapeDtypeStruct(x.shape, x.dt...]
where the time goes in v3:
time: 86.2 us; the launch traced here: 86 us
  Pallas kernels  85.2 us (99%)
    pallas_call x1, Pallas kernels, on_device(): pl.pallas_call(functools.partial(kernel, n_ctx, kv_heads, rows, kinds), o...  82.7 us
    pallas_call x1, Pallas kernels, hand_out(): pl.pallas_call(copy_kernel, out_shape=[jax.ShapeDtypeStruct(x.shape, x.dt...  2.55 us

profile of v3, /device:TPU:0, one launch (start us, length us, event | category | flops | bytes accessed | tf_op | source)
XLA Modules:
  0.0 86.0 jit_solution(11435272100527716031)
XLA Ops:
  0.6 82.7 %attention_fwd_bwd.1 = (bf16[160,2048]{1,0:T(8,128)(2,1)}, bf16[160,2048]{1,0:T(8,128)(2,1)}, bf16[160,512]{1,0:T(8,128)(2,1)}, bf16[160,512]{1,0:T(8,128)(2,1)}) custom-call(bf16[160,2048]{1,0:T(8,128)(2,1)} %q_ref.1, bf16[160,512]{1,0:T(8,128)(2,1)} %k_ref.1, bf16[160,512]{1,0:T(8,128)(2,1)} %v_ref.1, bf16[160,2048]{1,0:T(8,128)(2,1)} %g_ref.1, s32[16]{0:T(128)} %order_ref.1), custom_call_target="tpu_custom_call" | custom-call | tf_op jit(solution)/shard_map/attention_fwd_bwd/pallas_call | solution.py:498
  83.3 2.5 %hand_out.1 = (bf16[160,2048]{1,0:T(8,128)(2,1)}, bf16[160,2048]{1,0:T(8,128)(2,1)}, bf16[160,512]{1,0:T(8,128)(2,1)}, bf16[160,512]{1,0:T(8,128)(2,1)}) custom-call(bf16[160,2048]{1,0:T(8,128)(2,1)} %get-tuple-element.8.refs_0_, bf16[160,2048]{1,0:T(8,128)(2,1)} %get-tuple-element.9.refs_1_, bf16[160,512]{1,0:T(8,128)(2,1)} %get-tuple-element.10.refs_2_, ...), custom_call_target="tpu_custom_call" | custom-call | tf_op jit(solution)/shard_map/hand_out/pallas_call | solution.py:478

commit v4 on v3

--- a/solution.py
+++ b/solution.py
@@ -80,7 +80,7 @@
     kind_list = [Kind(i) for i in range(len(kinds))]
 
     def kind_of(h):
-        return kind_list[1 if h % 4 == 1 else 0]
+        return kind_list[h % len(kinds)]
 
     def block(slot):
         return pl.ds(pl.multiple_of(slot * span, span), span)
@@ -391,7 +391,7 @@
     def write_dq(h):
         write_rows(dq_ref, h, (dq_t[...] * scale).T.astype(jnp.bfloat16))
 
-    lag = 2
+    lag = 1
     ticks = []
     last_tick = lag * (kv_heads - 1) + max(ag_stages(h) for h in range(kv_heads))
     for t in range(last_tick):
@@ -425,9 +425,9 @@
         if h:
             load_queries(h)
         top = scores_pass(h)
-        run_ticks(lag * h + ag_stages(h) + 1)
+        run_ticks(done + 1)
         inverse, row_dot = weights_pass(h, top)
-        run_ticks(lag * h + ag_stages(h) + 2)
+        run_ticks(done + 1)
         advance()
         dq_t[...] = jnp.zeros_like(dq_t)
 
@@ -436,6 +436,7 @@
             return 0
 
         lax.fori_loop(1, kind.ns, away, 0)
+        run_ticks(done + 1)
         backward_group(h, kind.s, inverse, row_dot, False)
         advance()
         chains.append(rs_tasks(h))
@@ -491,7 +492,7 @@
     q_rows = GROUP * rows
     half_keys = n_ctx * rows // 2
     n0, n1 = line_lengths(n_ctx)
-    kinds = (0, 1) if kv_heads > 1 else (0,)
+    kinds = (0,)
     wide = 2 * HEAD_DIM
     longest = max(n0, n1)
     vmem = pl.BlockSpec(memory_space=pltpu.VMEM)

time: 86.2 us -> 81.1 us (0.941)
  Pallas kernels: 85.2 us -> 80.1 us
    pallas_call x1, Pallas kernels: 82.7 us -> 77.5 us  [on_device(): pl.pallas_call(functools.partial(kernel, n_ctx, kv_heads, rows, kinds), o...]
where the time goes in v4:
time: 81.1 us; the launch traced here: 80.9 us
  Pallas kernels  80.1 us (99%)
    pallas_call x1, Pallas kernels, on_device(): pl.pallas_call(functools.partial(kernel, n_ctx, kv_heads, rows, kinds), o...  77.5 us
    pallas_call x1, Pallas kernels, hand_out(): pl.pallas_call(copy_kernel, out_shape=[jax.ShapeDtypeStruct(x.shape, x.dt...  2.55 us

profile of v4, /device:TPU:0, one launch (start us, length us, event | category | flops | bytes accessed | tf_op | source)
XLA Modules:
  0.0 80.9 jit_solution(14930557277610815878)
XLA Ops:
  0.6 77.5 %attention_fwd_bwd.1 = (bf16[160,2048]{1,0:T(8,128)(2,1)}, bf16[160,2048]{1,0:T(8,128)(2,1)}, bf16[160,512]{1,0:T(8,128)(2,1)}, bf16[160,512]{1,0:T(8,128)(2,1)}) custom-call(bf16[160,2048]{1,0:T(8,128)(2,1)} %q_ref.1, bf16[160,512]{1,0:T(8,128)(2,1)} %k_ref.1, bf16[160,512]{1,0:T(8,128)(2,1)} %v_ref.1, bf16[160,2048]{1,0:T(8,128)(2,1)} %g_ref.1, s32[16]{0:T(128)} %order_ref.1), custom_call_target="tpu_custom_call" | custom-call | tf_op jit(solution)/shard_map/attention_fwd_bwd/pallas_call | solution.py:499
  78.2 2.5 %hand_out.1 = (bf16[160,2048]{1,0:T(8,128)(2,1)}, bf16[160,2048]{1,0:T(8,128)(2,1)}, bf16[160,512]{1,0:T(8,128)(2,1)}, bf16[160,512]{1,0:T(8,128)(2,1)}) custom-call(bf16[160,2048]{1,0:T(8,128)(2,1)} %get-tuple-element.8.refs_0_, bf16[160,2048]{1,0:T(8,128)(2,1)} %get-tuple-element.9.refs_1_, bf16[160,512]{1,0:T(8,128)(2,1)} %get-tuple-element.10.refs_2_, ...), custom_call_target="tpu_custom_call" | custom-call | tf_op jit(solution)/shard_map/hand_out/pallas_call | solution.py:479

commit v5 on v4

--- a/solution.py
+++ b/solution.py
@@ -311,7 +311,7 @@
     def rows_of(i, size):
         return pl.ds(pl.multiple_of(i * size, size), size)
 
-    tall = min(half_keys, 4 * span)
+    tall = min(half_keys, 8 * span)
 
     def fold(x, op):
         return op(x.reshape(x.shape[0] // 8, 8, x.shape[1]), axis=0)
@@ -367,13 +367,14 @@
     def backward_group(h, s, inverse, row_dot, send):
         kind = kind_of(h)
         where = rows_of(s, kind.nf * span)
+        low_grads = []
         for half, lanes in halves:
-            k, v = kv[h, half, where, 0:HEAD_DIM], kv[h, half, where, HEAD_DIM:]
+            v = kv[h, half, where, HEAD_DIM:]
             p = probs[half, where, lanes:] * inverse[:, lanes:]
             ds = (p * (dot_nt(v, gs[lanes:]) - row_dot[:, lanes:])).astype(jnp.bfloat16)
             acc[h, half, where, 0:HEAD_DIM] = dot_nn(ds, qs[lanes:])
             acc[h, half, where, HEAD_DIM:] = dot_nn(p.astype(jnp.bfloat16), gs[lanes:])
-            dq_t[:, lanes:] += dot_tn(k, ds)
+            low_grads.append(ds)
         if send:
             direction = jnp.where(s > kind.s, UP, DOWN)
             first = jnp.logical_or(
@@ -387,6 +388,9 @@
                 for b in range(kind.nf):
                     b = jnp.where(backwards, kind.nf - 1 - b, b)
                     s_pass_on(h, s * kind.nf + b, direction, True)
+
+        for (half, lanes), ds in zip(halves, low_grads):
+            dq_t[:, lanes:] += dot_tn(kv[h, half, where, 0:HEAD_DIM], ds)
 
     def write_dq(h):
         write_rows(dq_ref, h, (dq_t[...] * scale).T.astype(jnp.bfloat16))

time: 81.1 us -> 80.6 us (level)
  no operation moved by 1% of the time
where the time goes in v5:
time: 80.6 us; the launch traced here: 80.4 us
  Pallas kernels  79.6 us (99%)
    pallas_call x1, Pallas kernels, on_device(): pl.pallas_call(functools.partial(kernel, n_ctx, kv_heads, rows, kinds), o...  77.1 us
    pallas_call x1, Pallas kernels, hand_out(): pl.pallas_call(copy_kernel, out_shape=[jax.ShapeDtypeStruct(x.shape, x.dt...  2.55 us

profile of v5, /device:TPU:0, one launch (start us, length us, event | category | flops | bytes accessed | tf_op | source)
XLA Modules:
  0.0 80.4 jit_solution(7749074416103664801)
XLA Ops:
  0.6 77.1 %attention_fwd_bwd.1 = (bf16[160,2048]{1,0:T(8,128)(2,1)}, bf16[160,2048]{1,0:T(8,128)(2,1)}, bf16[160,512]{1,0:T(8,128)(2,1)}, bf16[160,512]{1,0:T(8,128)(2,1)}) custom-call(bf16[160,2048]{1,0:T(8,128)(2,1)} %q_ref.1, bf16[160,512]{1,0:T(8,128)(2,1)} %k_ref.1, bf16[160,512]{1,0:T(8,128)(2,1)} %v_ref.1, bf16[160,2048]{1,0:T(8,128)(2,1)} %g_ref.1, s32[16]{0:T(128)} %order_ref.1), custom_call_target="tpu_custom_call" | custom-call | tf_op jit(solution)/shard_map/attention_fwd_bwd/pallas_call | solution.py:503
  77.7 2.5 %hand_out.1 = (bf16[160,2048]{1,0:T(8,128)(2,1)}, bf16[160,2048]{1,0:T(8,128)(2,1)}, bf16[160,512]{1,0:T(8,128)(2,1)}, bf16[160,512]{1,0:T(8,128)(2,1)}) custom-call(bf16[160,2048]{1,0:T(8,128)(2,1)} %get-tuple-element.8.refs_0_, bf16[160,2048]{1,0:T(8,128)(2,1)} %get-tuple-element.9.refs_1_, bf16[160,512]{1,0:T(8,128)(2,1)} %get-tuple-element.10.refs_2_, ...), custom_call_target="tpu_custom_call" | custom-call | tf_op jit(solution)/shard_map/hand_out/pallas_call | solution.py:483

commit v6 on v5

--- a/solution.py
+++ b/solution.py
@@ -395,7 +395,7 @@
     def write_dq(h):
         write_rows(dq_ref, h, (dq_t[...] * scale).T.astype(jnp.bfloat16))
 
-    lag = 1
+    lag = 2
     ticks = []
     last_tick = lag * (kv_heads - 1) + max(ag_stages(h) for h in range(kv_heads))
     for t in range(last_tick):

time: 80.6 us -> 85.8 us (1.065)
  Pallas kernels: 79.6 us -> 84.8 us
    pallas_call x1, Pallas kernels: 77.1 us -> 82.2 us  [on_device(): pl.pallas_call(functools.partial(kernel, n_ctx, kv_heads, rows, kinds), o...]
where the time goes in v6:
time: 85.8 us; the launch traced here: 85.6 us
  Pallas kernels  84.8 us (99%)
    pallas_call x1, Pallas kernels, on_device(): pl.pallas_call(functools.partial(kernel, n_ctx, kv_heads, rows, kinds), o...  82.2 us
    pallas_call x1, Pallas kernels, hand_out(): pl.pallas_call(copy_kernel, out_shape=[jax.ShapeDtypeStruct(x.shape, x.dt...  2.55 us

profile of v6, /device:TPU:0, one launch (start us, length us, event | category | flops | bytes accessed | tf_op | source)
XLA Modules:
  0.0 85.6 jit_solution(12220525992476989187)
XLA Ops:
  0.6 82.2 %attention_fwd_bwd.1 = (bf16[160,2048]{1,0:T(8,128)(2,1)}, bf16[160,2048]{1,0:T(8,128)(2,1)}, bf16[160,512]{1,0:T(8,128)(2,1)}, bf16[160,512]{1,0:T(8,128)(2,1)}) custom-call(bf16[160,2048]{1,0:T(8,128)(2,1)} %q_ref.1, bf16[160,512]{1,0:T(8,128)(2,1)} %k_ref.1, bf16[160,512]{1,0:T(8,128)(2,1)} %v_ref.1, bf16[160,2048]{1,0:T(8,128)(2,1)} %g_ref.1, s32[16]{0:T(128)} %order_ref.1), custom_call_target="tpu_custom_call" | custom-call | tf_op jit(solution)/shard_map/attention_fwd_bwd/pallas_call | solution.py:503
  82.9 2.5 %hand_out.1 = (bf16[160,2048]{1,0:T(8,128)(2,1)}, bf16[160,2048]{1,0:T(8,128)(2,1)}, bf16[160,512]{1,0:T(8,128)(2,1)}, bf16[160,512]{1,0:T(8,128)(2,1)}) custom-call(bf16[160,2048]{1,0:T(8,128)(2,1)} %get-tuple-element.8.refs_0_, bf16[160,2048]{1,0:T(8,128)(2,1)} %get-tuple-element.9.refs_1_, bf16[160,512]{1,0:T(8,128)(2,1)} %get-tuple-element.10.refs_2_, ...), custom_call_target="tpu_custom_call" | custom-call | tf_op jit(solution)/shard_map/hand_out/pallas_call | solution.py:483
